TPU v7x, 32 devices: a whole 2x2x4 slice. The times are simulated.
32 devices in a mesh: groups: 2 (over y), long: 4 (over z), short: 4 (over x, core).
Axes of the slice: x: 2, y: 2, z: 4, core: 2. Of those that a mesh axis runs over, the one named last changes fastest.
Arguments:
- hidden_in: bfloat16 [128, 8192], P('groups', ('short', 'long')), parts along dimension 0, may hold values from -6 to 6
- mixer_gain: bfloat16 [8192], P(('short', 'long')), may hold values from 0.099609375 to 1.8984375
- mlp_gain: bfloat16 [8192], P(('short', 'long')), may hold values from 0.099609375 to 1.8984375
- gate_in_weight: bfloat16 [8192, 2, 8192], P('short', None, 'long'), may hold values from -0.0625 to 0.0625
- group_weight: bfloat16 [8192, 1024], P('short', 'long'), may hold values from -0.0625 to 0.0625
- step_weight: bfloat16 [8192, 128], P('short', 'long'), may hold values from -0.0625 to 0.0625
- step_bias: float32 [128], P(('long', 'short')), may hold values from -5 to 0
- decay_log: float32 [128], P(('long', 'short')), may hold values from 0 to 2.77
- skip_scale: float32 [128], P(('long', 'short')), may hold values from 0.5 to 2
- conv_weight: float32 [4, 8192], P(None, ('long', 'short')), may hold values from -3 to 3
- group_conv_weight: float32 [4, 1024], P(None, 'long'), may hold values from -3 to 3
- conv_state: float32 [128, 3, 8192], P('groups', None, ('long', 'short')), parts along dimension 0, may hold values from -6 to 6
- group_conv_state: float32 [128, 3, 1024], P('groups', None, 'long'), parts along dimension 0, may hold values from -6 to 6
- ssm_state: float32 [128, 128, 64, 128], P('groups', ('long', 'short')), parts along dimension 0, may hold values from -6 to 6
- norm_gain: float32 [8192], P(('long', 'short')), may hold values from 0.1 to 1.9
- out_weight: bfloat16 [8192, 8192], P('long', 'short'), may hold values from -0.09375 to 0.09375
- up_weight: bfloat16 [8192, 16384], P('short', 'long'), may hold values from -0.0625 to 0.0625
- down_weight: bfloat16 [16384, 8192], P('long', 'short'), may hold values from -0.0625 to 0.0625
Outputs:
- hidden_out: bfloat16 [128, 8192], P('groups', ('short', 'long')), parts along dimension 0
- new_ssm_state: float32 [128, 128, 64, 128], P('groups', ('long', 'short')), parts along dimension 0
- new_conv_state: float32 [128, 3, 8192], P('groups', None, ('long', 'short')), parts along dimension 0
- new_group_conv_state: float32 [128, 3, 1024], P('groups', None, 'long'), parts along dimension 0
There are 2 independent parts, one for each index of `groups`. A program takes and returns all parts, laid end to end along the dimension named above; an argument that names none is the same for every part. Nothing has to cross between parts.
All inputs are finite; a program needn't handle non-finite values.
Results may differ from a plain program's by a relative error of at most 0.0075.
Values may be sent and summed in bfloat16 or wider, within the bound.
No kernel may reach another device: no remote copies, remote signals or barrier semaphores. Data moves between devices by JAX's collectives and lax.ppermute only.
A program may use at most 192 MiB of HBM per device.

v0:
```python
import jax
import jax.numpy as jnp
from jax import lax
from jax.sharding import PartitionSpec as P

WIDTH = 8192
HEADS = 128
HEAD_DIM = 64
STATE = 128
GROUPS = 4
INNER = 8192


epsilon = 1e-05


def local(
    hidden_in,
    mixer_gain,
    mlp_gain,
    gate_in_weight,
    group_weight,
    step_weight,
    step_bias,
    decay_log,
    skip_scale,
    conv_weight,
    group_conv_weight,
    conv_state,
    group_conv_state,
    ssm_state,
    norm_gain,
    out_weight,
    up_weight,
    down_weight,
):
    gathered, gain_mixer, gain_mlp = (
        lax.all_gather(hidden_in, "long", axis=1, tiled=True),
        lax.all_gather(mixer_gain, "long", axis=0, tiled=True),
        lax.all_gather(mlp_gain, "long", axis=0, tiled=True),
    )
    features = gathered.astype(jnp.float32)
    scaled = (features * gain_mixer.astype(jnp.float32)).astype(jnp.bfloat16)
    partial_square = jnp.sum(features * features, axis=1)
    part_gates = jnp.einsum(
        "rd,dkc->rkc", scaled, gate_in_weight, preferred_element_type=jnp.float32
    )
    part_steps = jnp.dot(scaled, step_weight, preferred_element_type=jnp.float32)
    part_groups = jnp.dot(scaled, group_weight, preferred_element_type=jnp.float32)
    group_raw, total_square = lax.psum((part_groups, partial_square), "short")
    gate_in, step_raw = (
        lax.psum_scatter(part_gates, "short", scatter_dimension=2, tiled=True),
        lax.psum_scatter(part_steps, "short", scatter_dimension=1, tiled=True),
    )
    inverse = lax.rsqrt(total_square / WIDTH + epsilon)[:, None]
    gate_in = gate_in * inverse[:, :, None]
    step_raw = step_raw * inverse
    group_raw = group_raw * inverse
    window = jnp.concatenate([conv_state, gate_in[:, 1][:, None, :]], axis=1)
    mixer_input = jax.nn.silu(jnp.sum(window * conv_weight[None], axis=1))
    group_window = jnp.concatenate([group_conv_state, group_raw[:, None, :]], axis=1)
    group_act = jax.nn.silu(jnp.sum(group_window * group_conv_weight[None], axis=1))
    group_full = lax.all_gather(group_act, "long", axis=1, tiled=True)
    rows_here = gate_in.shape[0]
    heads_here = gate_in.shape[2] // HEAD_DIM
    first_head = (
        lax.axis_index("long") * lax.axis_size("short") + lax.axis_index("short")
    ) * heads_here
    group_index = first_head // (HEADS // GROUPS)
    state_in = lax.dynamic_slice_in_dim(group_full, group_index * STATE, STATE, 1)
    state_out = lax.dynamic_slice_in_dim(group_full, (GROUPS + group_index) * STATE, STATE, 1)
    step_size = jax.nn.softplus(step_raw + step_bias[None])
    decay = jnp.exp(-jnp.exp(decay_log)[None] * step_size)
    head_input = mixer_input.reshape(rows_here, heads_here, HEAD_DIM)
    new_state = (
        decay[:, :, None, None] * ssm_state
        + (step_size[:, :, None] * head_input)[:, :, :, None] * state_in[:, None, None, :]
    )
    readout = jnp.einsum("rhpn,rn->rhp", new_state, state_out, precision=lax.Precision.HIGHEST)
    readout = readout + skip_scale[None, :, None] * head_input
    readout = readout.reshape(rows_here, heads_here * HEAD_DIM) * jax.nn.silu(gate_in[:, 0])
    group_onehot = (jnp.arange(GROUPS) == group_index).astype(jnp.float32)
    local_square = jnp.sum(readout * readout, axis=1)
    group_totals = lax.psum(local_square[:, None] * group_onehot[None], ("long", "short"))
    group_mean = jnp.sum(group_totals * group_onehot[None], axis=1) / (INNER // GROUPS)
    normed = (readout * lax.rsqrt(group_mean + epsilon)[:, None] * norm_gain[None]).astype(
        jnp.bfloat16
    )
    normed_block = lax.all_gather(normed, "short", axis=1, tiled=True)
    part_mixed = jnp.dot(normed_block, out_weight, preferred_element_type=jnp.float32)
    mixed_own = lax.psum_scatter(part_mixed, "long", scatter_dimension=1, tiled=True)
    middle_own = (hidden_in.astype(jnp.float32) + mixed_own).astype(jnp.bfloat16)
    middle_block = lax.all_gather(middle_own, "long", axis=1, tiled=True)
    middle_full = middle_block.astype(jnp.float32)
    scaled_mid = (middle_full * gain_mlp.astype(jnp.float32)).astype(jnp.bfloat16)
    middle_square = lax.psum(jnp.sum(middle_full * middle_full, axis=1), "short")
    inverse_mid = lax.rsqrt(middle_square / WIDTH + epsilon)[:, None]
    part_upward = jnp.dot(scaled_mid, up_weight, preferred_element_type=jnp.float32)
    upward = lax.psum_scatter(part_upward, "short", scatter_dimension=1, tiled=True)
    active = jnp.square(jnp.maximum(upward * inverse_mid, 0.0)).astype(jnp.bfloat16)
    active_block = lax.all_gather(active, "short", axis=1, tiled=True)
    part_downward = jnp.dot(active_block, down_weight, preferred_element_type=jnp.float32)
    downward = lax.psum_scatter(part_downward, "long", scatter_dimension=1, tiled=True)
    hidden_out = (middle_own.astype(jnp.float32) + downward).astype(jnp.bfloat16)
    return (hidden_out, new_state, window[:, 1:], group_window[:, 1:])


def solution(mesh):
    placed = (
        P("groups", ("short", "long")),
        P(("short", "long")),
        P(("short", "long")),
        P("short", None, "long"),
        P("short", "long"),
        P("short", "long"),
        P(("long", "short")),
        P(("long", "short")),
        P(("long", "short")),
        P(None, ("long", "short")),
        P(None, "long"),
        P("groups", None, ("long", "short")),
        P("groups", None, "long"),
        P("groups", ("long", "short"), None, None),
        P(("long", "short")),
        P("long", "short"),
        P("short", "long"),
        P("long", "short"),
    )
    return jax.shard_map(
        local,
        mesh=mesh,
        in_specs=placed,
        out_specs=(
            P("groups", ("short", "long")),
            P("groups", ("long", "short"), None, None),
            P("groups", None, ("long", "short")),
            P("groups", None, "long"),
        ),
        check_vma=False,
    )
```

profile of v0, /device:TPU:0, one launch (start us, length us, event | category | flops | bytes accessed | tf_op | source)
XLA Modules:
  0.0 312.5 jit_solution(12842765831441090159)
XLA Ops:
  7.2 16.0 %all_gather.21 = bf16[64,2048]{1,0:T(8,128)(2,1)S(1)} all-gather(bf16[64,512]{1,0:T(8,128)(2,1)} %param.18), channel_id=1, replica_groups=mesh['groups'=2,'long'=4,'short'=4] {'long'}, dimensions={1}, use_global_device_ids=true | all-gather | bytes 327680 | tf_op jit(solution)/shard_map/all_gather | solution.py:38
  23.9 11.9 %all-gather = bf16[4,1,512]{2,1,0:T(2,128)(2,1)S(1)} all-gather(bf16[1,1,512]{2,1,0:T(2,128)(2,1)S(1)} %reshape.54), channel_id=1, replica_groups=mesh['groups'=2,'long'=4,'short'=4] {'long'}, dimensions={0}, use_global_device_ids=true | all-gather | bytes 5120 | tf_op jit(solution)/shard_map/all_gather | solution.py:39
  36.9 21.0 %fusion = f32[64,2,2048]{2,0,1:T(8,128)} fusion(bf16[2048,2,2048]{2,1,0:T(2,128)(2,1)} %param.21, bf16[64,2048]{1,0:T(8,128)(2,1)S(1)} %all_gather.21, f32[2048]{0:T(1024)S(1)} %bitcast.47), kind=kOutput, calls=%fused_computation | convolution fusion | flops 1074135040 | bytes 18096128 | tf_op jit(solution)/shard_map/rd,dkc->rkc/dot_general | solution.py:45
  59.7 10.6 %all-reduce.1 = (f32[64]{0:T(128)S(1)}, f32[64,32]{0,1:T(8,128)S(1)}) all-reduce(f32[64]{0:T(128)S(1)} %fusion.3, f32[64,32]{0,1:T(8,128)S(1)} %fusion.19), channel_id=1, replica_groups=mesh['groups'=2,'long'=4,'short'=4] {'short'}, use_global_device_ids=true, to_apply=%region_2.0 | all-reduce | flops 2112 | bytes 16896 | tf_op jit(solution)/shard_map/psum | solution.py:50
  71.6 14.0 %all_gather.23 = f32[64,1024]{1,0:T(8,128)S(1)} all-gather(f32[64,256]{1,0:T(8,128)S(1)} %divide_multiply_fusion.1), channel_id=1, replica_groups=mesh['groups'=2,'long'=4,'short'=4] {'long'}, dimensions={1}, use_global_device_ids=true | all-gather | bytes 327680 | tf_op jit(solution)/shard_map/all_gather | solution.py:63
  85.6 10.8 %reduce-scatter.5.cloned.1.call-done = f32[64,2,512]{2,0,1:T(8,128)} async-done(((f32[64,2,2048]{2,0,1:T(8,128)}), f32[64,2,512]{2,0,1:T(8,128)}) %reduce-scatter.5.cloned.1.call-update) | async-done | bytes 262160 | tf_op jit(solution)/shard_map/reduce_scatter | solution.py:52
  96.4 1.0 broadcast_multiply_fusion
  97.9 8.0 %multiply_add_fusion = f32[64,8,64,128]{3,2,1,0:T(8,128)S(1)} fusion(f32[64,8,64,128]{3,2,1,0:T(8,128)} %param.31, f32[64,128]{1,0:T(8,128)S(1)} %get-tuple-element.11, f32[64,8,64]{2,1,0:T(8,128)S(1)} %broadcast_multiply_fusion.1, f32[64,8]{1,0:T(8,128)S(1)} %copy.28), kind=kLoop, calls=%fused_computation.2 | loop fusion | flops 12582912 | bytes 33720320 | tf_op jit(solution)/shard_map/add | solution.py:76
  106.0 6.1 %copy-done.2 = f32[64,8,64,128]{3,2,1,0:T(8,128)} copy-done((f32[64,8,64,128]{3,2,1,0:T(8,128)}, f32[64,8,64,128]{3,2,1,0:T(8,128)S(1)}, u32[]{:S(2)}) %copy-start.2) | copy-done | bytes 16777240
  112.1 40.4 %fusion.30 = f32[64,1,8,64]{3,1,2,0:T(1,128)S(1)} fusion(f32[64,8,64,128]{3,2,1,0:T(8,128)S(1)} %multiply_add_fusion, f32[64,128,1,1]{1,2,3,0:T(1,128)S(1)} %bitcast.44), kind=kOutput, calls=%fused_computation.61 | convolution fusion | flops 50331648 | bytes 16941056 | tf_op jit(solution)/shard_map/rhpn,rn->rhp/dot_general | solution.py:79
  153.3 32.2 %psum.30 = f32[64,4]{0,1:T(4,128)S(1)} all-reduce(f32[64,4]{0,1:T(4,128)S(1)} %broadcast_multiply_fusion.2), channel_id=1, replica_groups=mesh['groups'=2,'long'=4,'short'=4] {'long','short'}, use_global_device_ids=true, to_apply=%region_8.9 | all-reduce | flops 256 | bytes 2048 | tf_op jit(solution)/shard_map/psum | solution.py:84
  185.8 5.8 %all_gather.24 = bf16[64,2048]{1,0:T(8,128)(2,1)S(1)} all-gather(bf16[64,512]{1,0:T(8,128)(2,1)S(1)} %fusion.27), channel_id=1, replica_groups=mesh['groups'=2,'long'=4,'short'=4] {'short'}, dimensions={1}, use_global_device_ids=true | all-gather | bytes 327680 | tf_op jit(solution)/shard_map/all_gather | solution.py:89
  191.6 5.7 %fusion.31 = f32[64,2048]{1,0:T(8,128)} fusion(bf16[64,2048]{1,0:T(8,128)(2,1)S(1)} %all_gather.24, bf16[2048,2048]{1,0:T(8,128)(2,1)} %param.33), kind=kOutput, calls=%fused_computation.62 | convolution fusion | flops 536870912 | bytes 9175040 | tf_op jit(solution)/shard_map/dot_general | solution.py:90
  197.4 11.9 %all-gather.1 = bf16[4,1,512]{2,1,0:T(2,128)(2,1)S(1)} all-gather(bf16[1,1,512]{2,1,0:T(2,128)(2,1)S(1)} %reshape.56), channel_id=1, replica_groups=mesh['groups'=2,'long'=4,'short'=4] {'long'}, dimensions={0}, use_global_device_ids=true | all-gather | bytes 5120 | tf_op jit(solution)/shard_map/all_gather | solution.py:40
  209.3 7.1 %reduce-scatter.7.cloned.1.call-done = f32[64,512]{1,0:T(8,128)} async-done(((f32[64,2048]{1,0:T(8,128)}), f32[64,512]{1,0:T(8,128)}) %reduce-scatter.7.cloned.1.call-update) | async-done | bytes 131088 | tf_op jit(solution)/shard_map/reduce_scatter | solution.py:91
  217.3 14.3 %all_gather.25 = bf16[64,2048]{1,0:T(8,128)(2,1)S(1)} all-gather(bf16[64,512]{1,0:T(8,128)(2,1)S(1)} %add_convert_fusion.1), channel_id=1, replica_groups=mesh['groups'=2,'long'=4,'short'=4] {'long'}, dimensions={1}, use_global_device_ids=true | all-gather | bytes 327680 | tf_op jit(solution)/shard_map/all_gather | solution.py:93
  231.6 9.9 %fusion.11 = f32[64,4096]{1,0:T(8,128)} fusion(bf16[2048,4096]{1,0:T(8,128)(2,1)} %param.34, bf16[64,2048]{1,0:T(8,128)(2,1)S(1)} %all_gather.25, f32[2048]{0:T(1024)S(1)} %bitcast.45), kind=kOutput, calls=%fused_computation.22 | convolution fusion | flops 1074135040 | bytes 18096128 | tf_op jit(solution)/shard_map/dot_general | solution.py:98
  241.7 5.7 %psum.31 = f32[64]{0:T(128)S(1)} all-reduce(f32[64]{0:T(128)S(1)} %fusion.5), channel_id=1, replica_groups=mesh['groups'=2,'long'=4,'short'=4] {'short'}, use_global_device_ids=true, to_apply=%region_13.14 | all-reduce | flops 64 | bytes 512 | tf_op jit(solution)/shard_map/psum | solution.py:96
  247.4 17.4 %reduce-scatter.9.cloned.1.call-done = f32[64,1024]{1,0:T(8,128)} async-done(((f32[64,4096]{1,0:T(8,128)}), f32[64,1024]{1,0:T(8,128)}) %reduce-scatter.9.cloned.1.call-update) | async-done | bytes 262160 | tf_op jit(solution)/shard_map/reduce_scatter | solution.py:99
  264.8 1.0 multiply_convert_fusion
  265.9 6.8 %all_gather.27 = bf16[64,4096]{1,0:T(8,128)(2,1)S(1)} all-gather(bf16[64,1024]{1,0:T(8,128)(2,1)S(1)} %multiply_convert_fusion), channel_id=1, replica_groups=mesh['groups'=2,'long'=4,'short'=4] {'short'}, dimensions={1}, use_global_device_ids=true | all-gather | bytes 655360 | tf_op jit(solution)/shard_map/all_gather | solution.py:101
  272.7 9.6 %fusion.32 = f32[64,2048]{1,0:T(8,128)} fusion(bf16[64,4096]{1,0:T(8,128)(2,1)S(1)} %all_gather.27, bf16[4096,2048]{1,0:T(8,128)(2,1)} %param.35), kind=kOutput, calls=%fused_computation.63 | convolution fusion | flops 1073741824 | bytes 17825792 | tf_op jit(solution)/shard_map/dot_general | solution.py:102
  283.8 20.7 %reduce-scatter.11.cloned.1.call-done = f32[64,512]{1,0:T(8,128)} async-done(((f32[64,2048]{1,0:T(8,128)}), f32[64,512]{1,0:T(8,128)}) %reduce-scatter.11.cloned.1.call-update) | async-done | bytes 131088 | tf_op jit(solution)/shard_map/reduce_scatter | solution.py:103
  304.4 1.5 add_convert_fusion
  (74 shorter events, 8.2 us)
Async XLA Ops:
  7.2 28.7 %copy-start = (bf16[2048,256]{1,0:T(8,128)(2,1)S(1)}, bf16[2048,256]{1,0:T(8,128)(2,1)}, u32[]{:S(2)}) copy-start(bf16[2048,256]{1,0:T(8,128)(2,1)} %param.22) | copy-start | bytes 3145732
  7.2 63.4 %all-reduce.4.cloned.1.call-start = ((), (), s32[]{:S(2)}) async-start(), calls=%async_computation.5 | async-start | bytes 131072 | tf_op jit(solution)/shard_map/psum | solution.py:50
  36.8 21.3 %copy-start.14 = (u32[32]{0:T(128)S(1)}, u32[32]{0:T(128)}, u32[]{:S(2)}) copy-start(u32[32]{0:T(128)} %constant.58) | copy-start | bytes 388
  36.8 22.6 %copy-start.12 = (bf16[2048,32]{0,1:T(8,128)(2,1)S(1)}, bf16[2048,32]{0,1:T(8,128)(2,1)}, u32[]{:S(2)}) copy-start(bf16[2048,32]{0,1:T(8,128)(2,1)} %param.23) | copy-start | bytes 393220
  36.8 33.4 %copy-start.13 = (f32[8]{0:T(128)S(1)}, f32[8]{0:T(128)}, u32[]{:S(2)}) copy-start(f32[8]{0:T(128)} %param.25) | copy-start | bytes 100
  36.8 33.4 %copy-start.11 = (f32[8]{0:T(128)S(1)}, f32[8]{0:T(128)}, u32[]{:S(2)}) copy-start(f32[8]{0:T(128)} %param.24) | copy-start | bytes 100
  36.8 34.7 %copy-start.4 = (f32[64,3,256]{2,0,1:T(8,128)S(1)}, f32[64,3,256]{2,0,1:T(8,128)}, u32[]{:S(2)}) copy-start(f32[64,3,256]{2,0,1:T(8,128)} %param.30) | copy-start | bytes 589828
  36.9 34.6 %copy-start.7 = (f32[4,256]{1,0:T(4,128)S(1)}, f32[4,256]{1,0:T(4,128)}, u32[]{:S(2)}) copy-start(f32[4,256]{1,0:T(4,128)} %param.28) | copy-start | bytes 12292
  36.9 60.6 %copy-start.3 = (f32[64,3,512]{2,0,1:T(8,128)S(1)}, f32[64,3,512]{2,0,1:T(8,128)}, u32[]{:S(2)}) copy-start(f32[64,3,512]{2,0,1:T(8,128)} %param.29) | copy-start | bytes 1179652
  36.9 60.6 %copy-start.6 = (f32[4,512]{1,0:T(4,128)S(1)}, f32[4,512]{1,0:T(4,128)}, u32[]{:S(2)}) copy-start(f32[4,512]{1,0:T(4,128)} %param.27) | copy-start | bytes 24580
  36.9 59.6 %reduce-scatter.5.cloned.1.call-start = ((), (), s32[]{:S(2)}) async-start(), calls=%async_computation.4 | async-start | bytes 1310720 | tf_op jit(solution)/shard_map/reduce_scatter | solution.py:52
  58.0 158.4 %reduce-scatter.7.cloned.1.call-start = ((), (), s32[]{:S(2)}) async-start(), calls=%async_computation.6 | async-start | bytes 655360 | tf_op jit(solution)/shard_map/reduce_scatter | solution.py:91
  105.9 6.2 %copy-start.2 = (f32[64,8,64,128]{3,2,1,0:T(8,128)}, f32[64,8,64,128]{3,2,1,0:T(8,128)S(1)}, u32[]{:S(2)}) copy-start(f32[64,8,64,128]{3,2,1,0:T(8,128)S(1)} %multiply_add_fusion) | copy-start | bytes 50331652
  106.0 46.6 %copy-start.10 = (f32[8]{0:T(128)S(1)}, f32[8]{0:T(128)}, u32[]{:S(2)}) copy-start(f32[8]{0:T(128)} %param.26) | copy-start | bytes 100
  106.0 79.7 %copy-start.8 = (f32[512]{0:T(512)S(1)}, f32[512]{0:T(512)}, u32[]{:S(2)}) copy-start(f32[512]{0:T(512)} %param.32) | copy-start | bytes 6148
  152.5 44.9 %copy-start.9 = (bf16[512]{0:T(512)(128)(2,1)S(1)}, bf16[512]{0:T(512)(128)(2,1)}, u32[]{:S(2)}) copy-start(bf16[512]{0:T(512)(128)(2,1)} %param.20) | copy-start | bytes 3076
  152.5 63.9 %copy-start.5 = (bf16[64,512]{1,0:T(8,128)(2,1)S(1)}, bf16[64,512]{1,0:T(8,128)(2,1)}, u32[]{:S(2)}) copy-start(bf16[64,512]{1,0:T(8,128)(2,1)} %param.18) | copy-start | bytes 196612
  197.3 67.5 %reduce-scatter.9.cloned.1.call-start = ((), (), s32[]{:S(2)}) async-start(), calls=%async_computation.7 | async-start | bytes 1310720 | tf_op jit(solution)/shard_map/reduce_scatter | solution.py:99
  231.6 74.4 %copy-start.1 = (bf16[2048,256]{1,0:T(8,128)(2,1)S(1)}, bf16[2048,256]{1,0:T(8,128)(2,1)}, u32[]{:S(2)}) copy-start(bf16[2048,256]{1,0:T(8,128)(2,1)} %param.22) | copy-start | bytes 3145732
  241.5 62.9 %reduce-scatter.11.cloned.1.call-start = ((), (), s32[]{:S(2)}) async-start(), calls=%async_computation.8 | async-start | bytes 655360 | tf_op jit(solution)/shard_map/reduce_scatter | solution.py:103
Sparse Core Ops, SparseCore 0:
  36.9 31.2 all-reduce.3
  71.5 24.8 reduce-scatter.4
  197.4 18.9 reduce-scatter.6
  241.6 23.1 reduce-scatter.8
  282.4 21.9 reduce-scatter.10
where the time goes:
time: 313 us
  blocking collectives  129 us (41%)
  matrix products  87.7 us (28%)
  waiting for transfers between devices  56.2 us (18%)
  other arithmetic  16.5 us (5%)
  between operations  14.8 us (5%)
  local copies, waits for them, and re-layouts  8.03 us (3%)
    dot_general x1, matrix products, local(): jnp.einsum('rhpn,rn->rhp', new_state, state_out, precision=lax.Precision....  40.4 us
    psum x1, blocking collectives, local(): lax.psum(local_square[:, None] * group_onehot[None], ('long', 'short'))  32.2 us
    dot_general x1, matrix products, local(): jnp.einsum('rd,dkc->rkc', scaled, gate_in_weight, preferred_element_type=...  21 us
    reduce_scatter x1, waiting for transfers between devices, local(): lax.psum_scatter(part_downward, 'long', scatter_dimension=1, tiled=True)  20.7 us
    reduce_scatter x1, waiting for transfers between devices, local(): lax.psum_scatter(part_upward, 'short', scatter_dimension=1, tiled=True)  17.4 us
    all_gather x1, blocking collectives, local(): lax.all_gather(hidden_in, 'long', axis=1, tiled=True)  16 us
    all_gather x1, blocking collectives, local(): middle_block = lax.all_gather(middle_own, 'long', axis=1, tiled=True)  14.3 us
    all_gather x1, blocking collectives, local(): group_full = lax.all_gather(group_act, 'long', axis=1, tiled=True)  14 us
  transfers between devices with their start and end apart: 5, of which 4 were waited for; matrix products, arithmetic and copies ran while one was open for 8% of the time, Pallas kernels for 0%

commit v1 on v0

v1 whole, which is shorter than its diff:
```python
import jax
import jax.numpy as jnp
from jax import lax
from jax.sharding import PartitionSpec as P

WIDTH = 8192
HEADS = 128
HEAD_DIM = 64
STATE = 128
GROUPS = 4
INNER = 8192

f32 = jnp.float32
bf16 = jnp.bfloat16
epsilon = 1e-05


def swap(value, axis, bits):
    size = lax.axis_size(axis)
    return lax.ppermute(value, axis, [(i, i ^ bits) for i in range(size)])


def in_order(blocks, index):
    stacked = jnp.stack(blocks)
    bit = 1
    while bit < len(blocks):
        shape = stacked.shape
        paired = stacked.reshape((-1, 2, bit) + shape[1:])
        stacked = jnp.where((index & bit) != 0, paired[:, ::-1], paired).reshape(shape)
        bit *= 2
    return stacked


def gather(value, axis):
    size = lax.axis_size(axis)
    blocks = [value] + [swap(value, axis, k) for k in range(1, size)]
    return in_order(blocks, lax.axis_index(axis))


def scatter_sum(parts, axis):
    size = lax.axis_size(axis)
    index = lax.axis_index(axis)
    total = lax.dynamic_index_in_dim(parts, index, 0, False)
    sent = parts.astype(bf16)
    for k in range(size - 1, 0, -1):
        block = lax.dynamic_index_in_dim(sent, index ^ k, 0, False)
        total = total + swap(block, axis, k).astype(f32)
    return total


def chip_scatter_sum(parts, axis):
    size = lax.axis_size(axis)
    index = lax.axis_index(axis)
    parts = parts.reshape((size // 2, 2) + parts.shape[1:])
    mine = lax.dynamic_index_in_dim(parts, index & 1, 1, False)
    other = lax.dynamic_index_in_dim(parts, (index & 1) ^ 1, 1, False)
    parts = mine + swap(other.astype(bf16), axis, 1).astype(f32)
    total = lax.dynamic_index_in_dim(parts, index // 2, 0, False)
    sent = parts.astype(bf16)
    for k in range(size // 2 - 1, 0, -1):
        block = lax.dynamic_index_in_dim(sent, (index // 2) ^ k, 0, False)
        total = total + swap(block, axis, 2 * k).astype(f32)
    return total


def total_over(value, axis):
    bit = 1
    while bit < lax.axis_size(axis):
        value = value + swap(value, axis, bit)
        bit *= 2
    return value


def split_pair(value):
    high = value.astype(bf16)
    return high, (value - high.astype(f32)).astype(bf16)


def with_square(block, square):
    high, low = split_pair(square)
    rows = block.shape[0]
    lanes = lax.broadcasted_iota(jnp.int32, (rows, 128), 1)
    tail = jnp.where(lanes == 0, high[:, None], jnp.where(lanes == 1, low[:, None], 0))
    return jnp.concatenate([block, tail.astype(bf16)], axis=1)


def square_of(tail):
    return tail[..., 0].astype(f32) + tail[..., 1].astype(f32)


def local(
    hidden_in,
    mixer_gain,
    mlp_gain,
    gate_in_weight,
    group_weight,
    step_weight,
    step_bias,
    decay_log,
    skip_scale,
    conv_weight,
    group_conv_weight,
    conv_state,
    group_conv_state,
    ssm_state,
    norm_gain,
    out_weight,
    up_weight,
    down_weight,
):
    rows = hidden_in.shape[0]
    longs, shorts = lax.axis_size("long"), lax.axis_size("short")
    at_long, at_short = lax.axis_index("long"), lax.axis_index("short")
    own = hidden_in.shape[1]

    features = hidden_in.astype(f32)
    scaled_own = (features * mixer_gain.astype(f32)).astype(bf16)
    blocks = gather(with_square(scaled_own, jnp.sum(features * features, axis=1)), "long")
    scaled = jnp.transpose(blocks[:, :, :own], (1, 0, 2)).reshape(rows, longs * own)
    square = jnp.sum(square_of(blocks[:, :, own:]), axis=0)

    part_groups = jnp.dot(scaled, group_weight, preferred_element_type=f32)
    part_steps = jnp.dot(scaled, step_weight, preferred_element_type=f32)
    small = total_over(jnp.concatenate([part_groups, part_steps, square[:, None]], axis=1), "short")
    wide = part_groups.shape[1]
    inverse = lax.rsqrt(small[:, -1:] / WIDTH + epsilon)
    group_raw = small[:, :wide] * inverse
    steps_here = part_steps.shape[1] // shorts
    step_raw = lax.dynamic_slice_in_dim(small, wide + at_short * steps_here, steps_here, 1) * inverse

    part_gates = jnp.einsum("rd,dkc->krc", scaled, gate_in_weight, preferred_element_type=f32)
    mixed_width = part_gates.shape[2] // shorts
    part_gates = jnp.transpose(part_gates.reshape(2, rows, shorts, mixed_width), (2, 0, 1, 3))
    gate_in = chip_scatter_sum(part_gates, "short") * inverse

    group_window = jnp.concatenate([group_conv_state, group_raw[:, None, :]], axis=1)
    group_act = jax.nn.silu(jnp.sum(group_window * group_conv_weight[None], axis=1))
    heads_here = mixed_width // HEAD_DIM
    first_head = (at_long * shorts + at_short) * heads_here
    group_index = first_head // (HEADS // GROUPS)
    group_full = gather(group_act, "long")
    group_full = jnp.transpose(group_full, (1, 0, 2)).reshape(rows, longs * wide)
    state_in = lax.dynamic_slice_in_dim(group_full, group_index * STATE, STATE, 1)
    state_out = lax.dynamic_slice_in_dim(group_full, (GROUPS + group_index) * STATE, STATE, 1)

    step_size = jax.nn.softplus(step_raw + step_bias[None])
    decay = jnp.exp(-jnp.exp(decay_log)[None] * step_size)
    window = jnp.concatenate([conv_state, gate_in[1][:, None, :]], axis=1)
    mixer_input = jax.nn.silu(jnp.sum(window * conv_weight[None], axis=1))
    head_input = mixer_input.reshape(rows, heads_here, HEAD_DIM)
    new_state = (
        decay[:, :, None, None] * ssm_state
        + (step_size[:, :, None] * head_input)[:, :, :, None] * state_in[:, None, None, :]
    )
    readout = jnp.sum(new_state * state_out[:, None, None, :], axis=-1)
    readout = readout + skip_scale[None, :, None] * head_input
    readout = readout.reshape(rows, heads_here * HEAD_DIM) * jax.nn.silu(gate_in[0])

    local_square = jnp.sum(readout * readout, axis=1)
    unscaled = (readout * norm_gain[None]).astype(bf16)
    blocks = gather(with_square(unscaled, local_square), "short")
    wide_own = unscaled.shape[1]
    normed = jnp.transpose(blocks[:, :, :wide_own], (1, 0, 2)).reshape(rows, shorts * wide_own)
    group_square = jnp.sum(square_of(blocks[:, :, wide_own:]), axis=0)
    if longs > GROUPS:
        mine = jnp.arange(GROUPS) == group_index
        totals = lax.psum(jnp.where(mine[None], group_square[:, None], 0.0), "long")
        group_square = jnp.sum(jnp.where(mine[None], totals, 0.0), axis=1)
    group_scale = lax.rsqrt(group_square / (INNER // GROUPS) + epsilon)
    part_mixed = jnp.dot(normed, out_weight, preferred_element_type=f32) * group_scale[:, None]
    part_mixed = jnp.transpose(part_mixed.reshape(rows, longs, own), (1, 0, 2))
    middle_own = (features + scatter_sum(part_mixed, "long")).astype(bf16)
    middle = middle_own.astype(f32)

    scaled_own = (middle * mlp_gain.astype(f32)).astype(bf16)
    blocks = gather(with_square(scaled_own, jnp.sum(middle * middle, axis=1)), "long")
    scaled_mid = jnp.transpose(blocks[:, :, :own], (1, 0, 2)).reshape(rows, longs * own)
    middle_square = jnp.sum(square_of(blocks[:, :, own:]), axis=0)

    part_up = jnp.dot(scaled_mid, up_weight, preferred_element_type=f32)
    half = part_up.shape[1] // 2
    core = at_short & 1
    mine = lax.dynamic_slice_in_dim(part_up, core * half, half, 1)
    other = lax.dynamic_slice_in_dim(part_up, (core ^ 1) * half, half, 1).astype(bf16)
    arrived = swap(with_square(other, middle_square), "short", 1)
    upward = mine + arrived[:, :half].astype(f32)
    middle_square = middle_square + square_of(arrived[:, half:])
    sent = with_square(upward.astype(bf16), middle_square)
    for k in range(1, shorts // 2):
        arrived = swap(sent, "short", 2 * k)
        upward = upward + arrived[:, :half].astype(f32)
        middle_square = middle_square + square_of(arrived[:, half:])
    inverse_mid = lax.rsqrt(middle_square / WIDTH + epsilon)[:, None]
    active_half = jnp.square(jnp.maximum(upward * inverse_mid, 0.0)).astype(bf16)
    pair = in_order([active_half, swap(active_half, "short", 1)], core)
    active = jnp.concatenate([pair[0], pair[1]], axis=1)

    part_down = jnp.dot(active, down_weight, preferred_element_type=f32)
    part_down = jnp.transpose(part_down.reshape(rows, longs, own), (1, 0, 2))
    hidden_out = (middle + scatter_sum(part_down, "long")).astype(bf16)
    return (hidden_out, new_state, window[:, 1:], group_window[:, 1:])


def solution(mesh):
    placed = (
        P("groups", ("short", "long")),
        P(("short", "long")),
        P(("short", "long")),
        P("short", None, "long"),
        P("short", "long"),
        P("short", "long"),
        P(("long", "short")),
        P(("long", "short")),
        P(("long", "short")),
        P(None, ("long", "short")),
        P(None, "long"),
        P("groups", None, ("long", "short")),
        P("groups", None, "long"),
        P("groups", ("long", "short"), None, None),
        P(("long", "short")),
        P("long", "short"),
        P("short", "long"),
        P("long", "short"),
    )
    return jax.shard_map(
        local,
        mesh=mesh,
        in_specs=placed,
        out_specs=(
            P("groups", ("short", "long")),
            P("groups", ("long", "short"), None, None),
            P("groups", None, ("long", "short")),
            P("groups", None, "long"),
        ),
        check_vma=False,
    )
```

time: 313 us -> 151 us (0.48)
  blocking collectives: 129 us -> 0 us
  matrix products: 87.7 us -> 39.3 us
  starting transfers between devices: 0.21 us -> 30.9 us
  between operations: 14.8 us -> 1.44 us
  waiting for transfers between devices: 56.2 us -> 44.4 us
  other arithmetic: 16.5 us -> 25.7 us
    all_gather x7 -> x0, blocking collectives: 80.7 us -> none  [the longest x1 16 us: local(): lax.all_gather(hidden_in, 'long', axis=1, tiled=True)]
    reduce_scatter x4 -> x0, waiting for transfers between devices: 56.1 us -> none  [the longest x1 20.7 us: local(): lax.psum_scatter(part_downward, 'long', scatter_dimension=1, tiled=True)]
    psum x3 -> x0, blocking collectives: 48.4 us -> none  [the longest x1 32.2 us: local(): lax.psum(local_square[:, None] * group_onehot[None], ('long', 'short'))]
    dot_general x7 -> x6, matrix products: 87.7 us -> 39.3 us  [the longest x1 15.2 us: local(): jnp.einsum('rd,dkc->krc', scaled, gate_in_weight, preferred_element_type=...]
    ppermute x0 -> x25, waiting for transfers between devices: none -> 44.4 us  [swap(): return lax.ppermute(value, axis, [(i, i ^ bits) for i in range(size)])]
    ppermute x0 -> x25, starting transfers between devices: none -> 30.9 us  [swap(): return lax.ppermute(value, axis, [(i, i ^ bits) for i in range(size)])]
    reduce_sum x3 -> x5, other arithmetic: 0.4 us -> 16.4 us  [the longest x1 14.6 us: local(): readout = jnp.sum(new_state * state_out[:, None, None, :], axis=-1)]
    add x1 -> x3, other arithmetic: 8 us -> 1.06 us  [the longest x2 0.95 us: total_over(): value = value + swap(value, axis, bit)]
  transfers between devices with their start and end apart: 5 -> 25, of which waited for: 4 -> 17; matrix products, arithmetic and copies ran while one was open for 8% -> 16% of each run, Pallas kernels for 0% -> 0%
where the time goes in v1:
time: 151 us
  waiting for transfers between devices  44.4 us (29%)
  matrix products  39.3 us (26%)
  starting transfers between devices  30.9 us (20%)
  other arithmetic  25.7 us (17%)
  local copies, waits for them, and re-layouts  8.82 us (6%)
    ppermute x25, waiting for transfers between devices, swap(): return lax.ppermute(value, axis, [(i, i ^ bits) for i in range(size)])  44.4 us
    ppermute x25, starting transfers between devices, swap(): return lax.ppermute(value, axis, [(i, i ^ bits) for i in range(size)])  30.9 us
    dot_general x1, matrix products, local(): jnp.einsum('rd,dkc->krc', scaled, gate_in_weight, preferred_element_type=...  15.2 us
    reduce_sum x1, other arithmetic, local(): readout = jnp.sum(new_state * state_out[:, None, None, :], axis=-1)  14.6 us
    dot_general x1, matrix products, local(): part_down = jnp.dot(active, down_weight, preferred_element_type=f32)  8.8 us
    dot_general x1, matrix products, local(): part_up = jnp.dot(scaled_mid, up_weight, preferred_element_type=f32)  8.78 us
    dot_general x1, matrix products, local(): jnp.dot(normed, out_weight, preferred_element_type=f32)  4.95 us
  transfers between devices with their start and end apart: 25, of which 17 were waited for; matrix products, arithmetic and copies ran while one was open for 16% of the time, Pallas kernels for 0%

profile of v1, /device:TPU:0, one launch (start us, length us, event | category | flops | bytes accessed | tf_op | source)
XLA Modules:
  0.0 150.5 jit_solution(17420026541402958104)
XLA Ops:
  2.5 3.1 %collective-permute-start = (bf16[64,640]{1,0:T(8,128)(2,1)S(1)}, bf16[64,640]{1,0:T(8,128)(2,1)S(1)}, u32[]{:S(2)}, u32[]{:S(2)}) collective-permute-start(bf16[64,640]{1,0:T(8,128)(2,1)S(1)} %get-tuple-element.41), channel_id=1, source_target_pairs={{0,4},{4,0},{8,12},{12,8},{1,5},{5,1},{9,13},{13,9},{2,6},{6,2},{1... | collective-permute-start | bytes 245768 | tf_op jit(solution)/shard_map/ppermute | solution.py:20
  5.6 2.6 %collective-permute-start.1 = (bf16[64,640]{1,0:T(8,128)(2,1)S(1)}, bf16[64,640]{1,0:T(8,128)(2,1)S(1)}, u32[]{:S(2)}, u32[]{:S(2)}) collective-permute-start(bf16[64,640]{1,0:T(8,128)(2,1)S(1)} %get-tuple-element.41), channel_id=1, source_target_pairs={{0,8},{4,12},{8,0},{12,4},{1,9},{5,13},{9,1},{13,5},{2,10},{6,14},... | collective-permute-start | bytes 245768 | tf_op jit(solution)/shard_map/ppermute | solution.py:20
  9.7 5.1 %collective-permute-done.1 = bf16[64,640]{1,0:T(8,128)(2,1)S(1)} collective-permute-done((bf16[64,640]{1,0:T(8,128)(2,1)S(1)}, bf16[64,640]{1,0:T(8,128)(2,1)S(1)}, u32[]{:S(2)}, u32[]{:S(2)}) %collective-permute-start.1) | collective-permute-done | bytes 81952 | tf_op jit(solution)/shard_map/ppermute | solution.py:20
  17.9 15.2 %fusion.2 = f32[2,64,2048]{2,1,0:T(8,128)S(1)} fusion(bf16[64,2048,1]{1,0,2:T(8,128)(2,1)S(1)} %reshape.217, bf16[2048,2,2048]{2,1,0:T(2,128)(2,1)} %param.21), kind=kOutput, calls=%fused_computation.4 | convolution fusion | flops 1073741824 | bytes 18087936 | tf_op jit(solution)/shard_map/rd,dkc->krc/dot_general | solution.py:131
  38.8 3.8 %collective-permute-done.4 = f32[64,289]{0,1:T(8,128)S(1)} collective-permute-done((f32[64,289]{0,1:T(8,128)S(1)}, f32[64,289]{0,1:T(8,128)S(1)}, u32[]{:S(2)}, u32[]{:S(2)}) %collective-permute-start.4) | collective-permute-done | bytes 74016 | tf_op jit(solution)/shard_map/ppermute | solution.py:20
  44.4 1.6 %collective-permute-start.8 = (f32[64,256]{1,0:T(8,128)S(1)}, f32[64,256]{1,0:T(8,128)S(1)}, u32[]{:S(2)}, u32[]{:S(2)}) collective-permute-start(f32[64,256]{1,0:T(8,128)S(1)} %divide_multiply_fusion), channel_id=1, source_target_pairs={{0,8},{4,12},{8,0},{12,4},{1,9},{5,13},{9,1},{13,5},{2,10},{6,14},... | collective-permute-start | bytes 196616 | tf_op jit(solution)/shard_map/ppermute | solution.py:20
  47.9 3.1 %collective-permute-done.8 = f32[64,256]{1,0:T(8,128)S(1)} collective-permute-done((f32[64,256]{1,0:T(8,128)S(1)}, f32[64,256]{1,0:T(8,128)S(1)}, u32[]{:S(2)}, u32[]{:S(2)}) %collective-permute-start.8) | collective-permute-done | bytes 65568 | tf_op jit(solution)/shard_map/ppermute | solution.py:20
  55.7 3.1 %collective-permute-done.6 = bf16[2,64,512]{2,1,0:T(8,128)(2,1)S(1)} collective-permute-done((bf16[2,64,512]{2,1,0:T(8,128)(2,1)S(1)}, bf16[2,64,512]{2,1,0:T(8,128)(2,1)S(1)}, u32[]{:S(2)}, u32[]{:S(2)}) %collective-permute-start.6) | collective-permute-done | bytes 131104 | tf_op jit(solution)/shard_map/ppermute | solution.py:20
  59.2 14.6 %multiply_reduce_fusion = (f32[64,8,64]{2,1,0:T(8,128)S(1)}, f32[64,8,64,128]{3,2,1,0:T(8,128)}) fusion(f32[64,128]{1,0:T(8,128)S(1)} %get-tuple-element.33, f32[64,128]{1,0:T(8,128)S(1)} %get-tuple-element.32, f32[64,8,64]{2,1,0:T(8,128)S(1)} %multiply_multiply_fusion, f32[64,8,64,128]{3,2,1,0:T(8,128)} %param.31, f32[64,8]{1,0:T(8,128)S(1)} %copy.71), kind=kLoop, calls=%fused_computation.2 | loop fusion | flops 20938752 | bytes 33884160 | tf_op jit(solution)/shard_map/reduce_sum | solution.py:155
  76.2 3.3 %collective-permute-done.11 = bf16[64,640]{1,0:T(8,128)(2,1)S(1)} collective-permute-done((bf16[64,640]{1,0:T(8,128)(2,1)S(1)}, bf16[64,640]{1,0:T(8,128)(2,1)S(1)}, u32[]{:S(2)}, u32[]{:S(2)}) %collective-permute-start.11) | collective-permute-done | bytes 81952 | tf_op jit(solution)/shard_map/ppermute | solution.py:20
  81.8 5.0 %convolution_multiply_fusion = f32[64,2048]{1,0:T(8,128)S(1)} fusion(bf16[64,2048]{1,0:T(8,128)(2,1)S(1)} %bitcast.161, bf16[2048,2048]{1,0:T(8,128)(2,1)} %param.33, f32[64]{0:T(128)S(1)} %add_rsqrt_fusion), kind=kOutput, calls=%fused_computation.5 | convolution fusion | flops 537001984 | bytes 9175296 | tf_op jit(solution)/shard_map/dot_general | solution.py:170
  87.2 2.2 %collective-permute-start.13 = (bf16[64,512]{1,0:T(8,128)(2,1)S(1)}, bf16[64,512]{1,0:T(8,128)(2,1)S(1)}, u32[]{:S(2)}, u32[]{:S(2)}) collective-permute-start(bf16[64,512]{1,0:T(8,128)(2,1)S(1)} %get-tuple-element.29), channel_id=1, source_target_pairs={{0,12},{4,8},{8,4},{12,0},{1,13},{5,9},{9,5},{13,1},{2,14},{6,10},... | collective-permute-start | bytes 196616 | tf_op jit(solution)/shard_map/ppermute | solution.py:20
  89.5 2.1 %collective-permute-start.15 = (bf16[64,512]{1,0:T(8,128)(2,1)S(1)}, bf16[64,512]{1,0:T(8,128)(2,1)S(1)}, u32[]{:S(2)}, u32[]{:S(2)}) collective-permute-start(bf16[64,512]{1,0:T(8,128)(2,1)S(1)} %get-tuple-element.30), channel_id=1, source_target_pairs={{0,4},{4,0},{8,12},{12,8},{1,5},{5,1},{9,13},{13,9},{2,6},{6,2},{1... | collective-permute-start | bytes 196616 | tf_op jit(solution)/shard_map/ppermute | solution.py:20
  91.7 2.2 %collective-permute-done.13 = bf16[64,512]{1,0:T(8,128)(2,1)S(1)} collective-permute-done((bf16[64,512]{1,0:T(8,128)(2,1)S(1)}, bf16[64,512]{1,0:T(8,128)(2,1)S(1)}, u32[]{:S(2)}, u32[]{:S(2)}) %collective-permute-start.13) | collective-permute-done | bytes 65568 | tf_op jit(solution)/shard_map/ppermute | solution.py:20
  94.0 2.0 %collective-permute-done.14 = bf16[64,512]{1,0:T(8,128)(2,1)S(1)} collective-permute-done((bf16[64,512]{1,0:T(8,128)(2,1)S(1)}, bf16[64,512]{1,0:T(8,128)(2,1)S(1)}, u32[]{:S(2)}, u32[]{:S(2)}) %collective-permute-start.14) | collective-permute-done | bytes 65568 | tf_op jit(solution)/shard_map/ppermute | solution.py:20
  96.7 2.7 %collective-permute-start.17 = (bf16[64,640]{1,0:T(8,128)(2,1)S(1)}, bf16[64,640]{1,0:T(8,128)(2,1)S(1)}, u32[]{:S(2)}, u32[]{:S(2)}) collective-permute-start(bf16[64,640]{1,0:T(8,128)(2,1)S(1)} %get-tuple-element.37), channel_id=1, source_target_pairs={{0,8},{4,12},{8,0},{12,4},{1,9},{5,13},{9,1},{13,5},{2,10},{6,14},... | collective-permute-start | bytes 245768 | tf_op jit(solution)/shard_map/ppermute | solution.py:20
  101.7 4.6 %collective-permute-done.17 = bf16[64,640]{1,0:T(8,128)(2,1)S(1)} collective-permute-done((bf16[64,640]{1,0:T(8,128)(2,1)S(1)}, bf16[64,640]{1,0:T(8,128)(2,1)S(1)}, u32[]{:S(2)}, u32[]{:S(2)}) %collective-permute-start.17) | collective-permute-done | bytes 81952 | tf_op jit(solution)/shard_map/ppermute | solution.py:20
  107.5 8.8 %fusion.61 = f32[64,4096]{1,0:T(8,128)S(1)} fusion(bf16[64,2048]{1,0:T(8,128)(2,1)S(1)} %bitcast.168, bf16[2048,4096]{1,0:T(8,128)(2,1)} %param.34), kind=kOutput, calls=%fused_computation.153 | convolution fusion | flops 1073741824 | bytes 18087936 | tf_op jit(solution)/shard_map/dot_general | solution.py:180
  118.5 1.6 %collective-permute-start.20 = (bf16[64,2176]{1,0:T(8,128)(2,1)S(1)}, bf16[64,2176]{1,0:T(8,128)(2,1)S(1)}, u32[]{:S(2)}, u32[]{:S(2)}) collective-permute-start(bf16[64,2176]{1,0:T(8,128)(2,1)S(1)} %pad_maximum_fusion.7), channel_id=1, source_target_pairs={{0,2},{1,3},{2,0},{3,1},{4,6},{5,7},{6,4},{7,5},{8,10},{9,11},{10,... | collective-permute-start | bytes 835592 | tf_op jit(solution)/shard_map/ppermute | solution.py:20
  120.1 7.2 %collective-permute-done.20 = bf16[64,2176]{1,0:T(8,128)(2,1)S(1)} collective-permute-done((bf16[64,2176]{1,0:T(8,128)(2,1)S(1)}, bf16[64,2176]{1,0:T(8,128)(2,1)S(1)}, u32[]{:S(2)}, u32[]{:S(2)}) %collective-permute-start.20) | collective-permute-done | bytes 278560 | tf_op jit(solution)/shard_map/ppermute | solution.py:20
  131.0 8.8 %fusion.7 = f32[64,2048]{1,0:T(8,128)S(1)} fusion(bf16[4096,2048]{1,0:T(8,128)(2,1)} %param.35, bf16[64,2048]{1,0:T(8,128)(2,1)S(1)} %slice_bitcast_fusion, bf16[64,2048]{1,0:T(8,128)(2,1)S(1)} %slice_bitcast_fusion.1), kind=kOutput, calls=%fused_computation.15 | convolution fusion | flops 1074790400 | bytes 17825792 | tf_op jit(solution)/shard_map/dot_general | solution.py:198
  140.3 2.1 %collective-permute-start.22 = (bf16[64,512]{1,0:T(8,128)(2,1)S(1)}, bf16[64,512]{1,0:T(8,128)(2,1)S(1)}, u32[]{:S(2)}, u32[]{:S(2)}) collective-permute-start(bf16[64,512]{1,0:T(8,128)(2,1)S(1)} %get-tuple-element.26), channel_id=1, source_target_pairs={{0,12},{4,8},{8,4},{12,0},{1,13},{5,9},{9,5},{13,1},{2,14},{6,10},... | collective-permute-start | bytes 196616 | tf_op jit(solution)/shard_map/ppermute | solution.py:20
  144.8 2.3 %collective-permute-done.22 = bf16[64,512]{1,0:T(8,128)(2,1)S(1)} collective-permute-done((bf16[64,512]{1,0:T(8,128)(2,1)S(1)}, bf16[64,512]{1,0:T(8,128)(2,1)S(1)}, u32[]{:S(2)}, u32[]{:S(2)}) %collective-permute-start.22) | collective-permute-done | bytes 65568 | tf_op jit(solution)/shard_map/ppermute | solution.py:20
  147.1 2.7 %collective-permute-done.23 = bf16[64,512]{1,0:T(8,128)(2,1)S(1)} collective-permute-done((bf16[64,512]{1,0:T(8,128)(2,1)S(1)}, bf16[64,512]{1,0:T(8,128)(2,1)S(1)}, u32[]{:S(2)}, u32[]{:S(2)}) %collective-permute-start.23) | collective-permute-done | bytes 65568 | tf_op jit(solution)/shard_map/ppermute | solution.py:20
  (170 shorter events, 39.5 us)
Async XLA Ops:
  2.5 7.2 %collective-permute-start = (bf16[64,640]{1,0:T(8,128)(2,1)S(1)}, bf16[64,640]{1,0:T(8,128)(2,1)S(1)}, u32[]{:S(2)}, u32[]{:S(2)}) collective-permute-start(bf16[64,640]{1,0:T(8,128)(2,1)S(1)} %get-tuple-element.41), channel_id=1, source_target_pairs={{0,4},{4,0},{8,12},{12,8},{1,5},{5,1},{9,13},{13,9},{2,6},{6,2},{1... | collective-permute-start | bytes 245768 | tf_op jit(solution)/shard_map/ppermute | solution.py:20
  5.6 9.2 %collective-permute-start.1 = (bf16[64,640]{1,0:T(8,128)(2,1)S(1)}, bf16[64,640]{1,0:T(8,128)(2,1)S(1)}, u32[]{:S(2)}, u32[]{:S(2)}) collective-permute-start(bf16[64,640]{1,0:T(8,128)(2,1)S(1)} %get-tuple-element.41), channel_id=1, source_target_pairs={{0,8},{4,12},{8,0},{12,4},{1,9},{5,13},{9,1},{13,5},{2,10},{6,14},... | collective-permute-start | bytes 245768 | tf_op jit(solution)/shard_map/ppermute | solution.py:20
  8.2 6.6 %collective-permute-start.2 = (bf16[64,640]{1,0:T(8,128)(2,1)S(1)}, bf16[64,640]{1,0:T(8,128)(2,1)S(1)}, u32[]{:S(2)}, u32[]{:S(2)}) collective-permute-start(bf16[64,640]{1,0:T(8,128)(2,1)S(1)} %get-tuple-element.41), channel_id=1, source_target_pairs={{0,12},{4,8},{8,4},{12,0},{1,13},{5,9},{9,5},{13,1},{2,14},{6,10},... | collective-permute-start | bytes 245768 | tf_op jit(solution)/shard_map/ppermute | solution.py:20
  17.6 18.2 %collective-permute-start.3 = (f32[64,289]{0,1:T(8,128)S(1)}, f32[64,289]{0,1:T(8,128)}, u32[]{:S(2)}, u32[]{:S(2)}) collective-permute-start(f32[64,289]{0,1:T(8,128)S(1)} %pad_maximum_fusion.9), channel_id=1, source_target_pairs={{0,1},{1,0},{2,3},{3,2},{4,5},{5,4},{6,7},{7,6},{8,9},{9,8},{10,11... | collective-permute-start | bytes 221960 | tf_op jit(solution)/shard_map/ppermute | solution.py:20
  35.2 18.3 %collective-permute-start.5 = (bf16[2,2,64,512]{3,2,1,0:T(8,128)(2,1)S(1)}, bf16[2,2,64,512]{3,2,1,0:T(8,128)(2,1)S(1)}, u32[]{:S(2)}, u32[]{:S(2)}) collective-permute-start(bf16[2,2,64,512]{3,2,1,0:T(8,128)(2,1)S(1)} %bitcast.179), channel_id=1, source_target_pairs={{0,1},{1,0},{2,3},{3,2},{4,5},{5,4},{6,7},{7,6},{8,9},{9,8},{10,11... | collective-permute-start | bytes 786440 | tf_op jit(solution)/shard_map/ppermute | solution.py:20
  36.7 5.9 %collective-permute-start.4 = (f32[64,289]{0,1:T(8,128)S(1)}, f32[64,289]{0,1:T(8,128)S(1)}, u32[]{:S(2)}, u32[]{:S(2)}) collective-permute-start(f32[64,289]{0,1:T(8,128)S(1)} %fusion.47), channel_id=1, source_target_pairs={{0,2},{1,3},{2,0},{3,1},{4,6},{5,7},{6,4},{7,5},{8,10},{9,11},{10,... | collective-permute-start | bytes 221960 | tf_op jit(solution)/shard_map/ppermute | solution.py:20
  42.9 5.0 %collective-permute-start.7 = (f32[64,256]{1,0:T(8,128)S(1)}, f32[64,256]{1,0:T(8,128)S(1)}, u32[]{:S(2)}, u32[]{:S(2)}) collective-permute-start(f32[64,256]{1,0:T(8,128)S(1)} %divide_multiply_fusion), channel_id=1, source_target_pairs={{0,4},{4,0},{8,12},{12,8},{1,5},{5,1},{9,13},{13,9},{2,6},{6,2},{1... | collective-permute-start | bytes 196616 | tf_op jit(solution)/shard_map/ppermute | solution.py:20
  44.4 6.6 %collective-permute-start.8 = (f32[64,256]{1,0:T(8,128)S(1)}, f32[64,256]{1,0:T(8,128)S(1)}, u32[]{:S(2)}, u32[]{:S(2)}) collective-permute-start(f32[64,256]{1,0:T(8,128)S(1)} %divide_multiply_fusion), channel_id=1, source_target_pairs={{0,8},{4,12},{8,0},{12,4},{1,9},{5,13},{9,1},{13,5},{2,10},{6,14},... | collective-permute-start | bytes 196616 | tf_op jit(solution)/shard_map/ppermute | solution.py:20
  46.0 6.2 %collective-permute-start.9 = (f32[64,256]{1,0:T(8,128)S(1)}, f32[64,256]{1,0:T(8,128)S(1)}, u32[]{:S(2)}, u32[]{:S(2)}) collective-permute-start(f32[64,256]{1,0:T(8,128)S(1)} %divide_multiply_fusion), channel_id=1, source_target_pairs={{0,12},{4,8},{8,4},{12,0},{1,13},{5,9},{9,5},{13,1},{2,14},{6,10},... | collective-permute-start | bytes 196616 | tf_op jit(solution)/shard_map/ppermute | solution.py:20
  53.7 5.0 %collective-permute-start.6 = (bf16[2,64,512]{2,1,0:T(8,128)(2,1)S(1)}, bf16[2,64,512]{2,1,0:T(8,128)(2,1)S(1)}, u32[]{:S(2)}, u32[]{:S(2)}) collective-permute-start(bf16[2,64,512]{2,1,0:T(8,128)(2,1)S(1)} %fusion.29), channel_id=1, source_target_pairs={{0,2},{1,3},{2,0},{3,1},{4,6},{5,7},{6,4},{7,5},{8,10},{9,11},{10,... | collective-permute-start | bytes 393224 | tf_op jit(solution)/shard_map/ppermute | solution.py:20
  74.3 1.9 %collective-permute-start.10 = (bf16[64,640]{1,0:T(8,128)(2,1)S(1)}, bf16[64,640]{1,0:T(8,128)(2,1)S(1)}, u32[]{:S(2)}, u32[]{:S(2)}) collective-permute-start(bf16[64,640]{1,0:T(8,128)(2,1)S(1)} %get-tuple-element.39), channel_id=1, source_target_pairs={{0,1},{1,0},{2,3},{3,2},{4,5},{5,4},{6,7},{7,6},{8,9},{9,8},{10,11... | collective-permute-start | bytes 245768 | tf_op jit(solution)/shard_map/ppermute | solution.py:20
  74.3 5.2 %collective-permute-start.11 = (bf16[64,640]{1,0:T(8,128)(2,1)S(1)}, bf16[64,640]{1,0:T(8,128)(2,1)S(1)}, u32[]{:S(2)}, u32[]{:S(2)}) collective-permute-start(bf16[64,640]{1,0:T(8,128)(2,1)S(1)} %get-tuple-element.39), channel_id=1, source_target_pairs={{0,2},{1,3},{2,0},{3,1},{4,6},{5,7},{6,4},{7,5},{8,10},{9,11},{10,... | collective-permute-start | bytes 245768 | tf_op jit(solution)/shard_map/ppermute | solution.py:20
  75.9 4.7 %collective-permute-start.12 = (bf16[64,640]{1,0:T(8,128)(2,1)S(1)}, bf16[64,640]{1,0:T(8,128)(2,1)S(1)}, u32[]{:S(2)}, u32[]{:S(2)}) collective-permute-start(bf16[64,640]{1,0:T(8,128)(2,1)S(1)} %get-tuple-element.39), channel_id=1, source_target_pairs={{0,3},{1,2},{2,1},{3,0},{4,7},{5,6},{6,5},{7,4},{8,11},{9,10},{10,... | collective-permute-start | bytes 245768 | tf_op jit(solution)/shard_map/ppermute | solution.py:20
  87.2 6.8 %collective-permute-start.13 = (bf16[64,512]{1,0:T(8,128)(2,1)S(1)}, bf16[64,512]{1,0:T(8,128)(2,1)S(1)}, u32[]{:S(2)}, u32[]{:S(2)}) collective-permute-start(bf16[64,512]{1,0:T(8,128)(2,1)S(1)} %get-tuple-element.29), channel_id=1, source_target_pairs={{0,12},{4,8},{8,4},{12,0},{1,13},{5,9},{9,5},{13,1},{2,14},{6,10},... | collective-permute-start | bytes 196616 | tf_op jit(solution)/shard_map/ppermute | solution.py:20
  89.3 6.7 %collective-permute-start.14 = (bf16[64,512]{1,0:T(8,128)(2,1)S(1)}, bf16[64,512]{1,0:T(8,128)(2,1)S(1)}, u32[]{:S(2)}, u32[]{:S(2)}) collective-permute-start(bf16[64,512]{1,0:T(8,128)(2,1)S(1)} %get-tuple-element.31), channel_id=1, source_target_pairs={{0,8},{4,12},{8,0},{12,4},{1,9},{5,13},{9,1},{13,5},{2,10},{6,14},... | collective-permute-start | bytes 196616 | tf_op jit(solution)/shard_map/ppermute | solution.py:20
  89.5 6.5 %collective-permute-start.15 = (bf16[64,512]{1,0:T(8,128)(2,1)S(1)}, bf16[64,512]{1,0:T(8,128)(2,1)S(1)}, u32[]{:S(2)}, u32[]{:S(2)}) collective-permute-start(bf16[64,512]{1,0:T(8,128)(2,1)S(1)} %get-tuple-element.30), channel_id=1, source_target_pairs={{0,4},{4,0},{8,12},{12,8},{1,5},{5,1},{9,13},{13,9},{2,6},{6,2},{1... | collective-permute-start | bytes 196616 | tf_op jit(solution)/shard_map/ppermute | solution.py:20
  96.3 5.4 %collective-permute-start.16 = (bf16[64,640]{1,0:T(8,128)(2,1)S(1)}, bf16[64,640]{1,0:T(8,128)(2,1)S(1)}, u32[]{:S(2)}, u32[]{:S(2)}) collective-permute-start(bf16[64,640]{1,0:T(8,128)(2,1)S(1)} %get-tuple-element.37), channel_id=1, source_target_pairs={{0,4},{4,0},{8,12},{12,8},{1,5},{5,1},{9,13},{13,9},{2,6},{6,2},{1... | collective-permute-start | bytes 245768 | tf_op jit(solution)/shard_map/ppermute | solution.py:20
  96.7 9.6 %collective-permute-start.17 = (bf16[64,640]{1,0:T(8,128)(2,1)S(1)}, bf16[64,640]{1,0:T(8,128)(2,1)S(1)}, u32[]{:S(2)}, u32[]{:S(2)}) collective-permute-start(bf16[64,640]{1,0:T(8,128)(2,1)S(1)} %get-tuple-element.37), channel_id=1, source_target_pairs={{0,8},{4,12},{8,0},{12,4},{1,9},{5,13},{9,1},{13,5},{2,10},{6,14},... | collective-permute-start | bytes 245768 | tf_op jit(solution)/shard_map/ppermute | solution.py:20
  99.4 7.0 %collective-permute-start.18 = (bf16[64,640]{1,0:T(8,128)(2,1)S(1)}, bf16[64,640]{1,0:T(8,128)(2,1)S(1)}, u32[]{:S(2)}, u32[]{:S(2)}) collective-permute-start(bf16[64,640]{1,0:T(8,128)(2,1)S(1)} %get-tuple-element.37), channel_id=1, source_target_pairs={{0,12},{4,8},{8,4},{12,0},{1,13},{5,9},{9,5},{13,1},{2,14},{6,10},... | collective-permute-start | bytes 245768 | tf_op jit(solution)/shard_map/ppermute | solution.py:20
  116.4 1.6 %collective-permute-start.19 = (bf16[64,2176]{1,0:T(8,128)(2,1)S(1)}, bf16[64,2176]{1,0:T(8,128)(2,1)S(1)}, u32[]{:S(2)}, u32[]{:S(2)}) collective-permute-start(bf16[64,2176]{1,0:T(8,128)(2,1)S(1)} %pad_maximum_fusion.6), channel_id=1, source_target_pairs={{0,1},{1,0},{2,3},{3,2},{4,5},{5,4},{6,7},{7,6},{8,9},{9,8},{10,11... | collective-permute-start | bytes 835592 | tf_op jit(solution)/shard_map/ppermute | solution.py:20
  118.5 8.8 %collective-permute-start.20 = (bf16[64,2176]{1,0:T(8,128)(2,1)S(1)}, bf16[64,2176]{1,0:T(8,128)(2,1)S(1)}, u32[]{:S(2)}, u32[]{:S(2)}) collective-permute-start(bf16[64,2176]{1,0:T(8,128)(2,1)S(1)} %pad_maximum_fusion.7), channel_id=1, source_target_pairs={{0,2},{1,3},{2,0},{3,1},{4,6},{5,7},{6,4},{7,5},{8,10},{9,11},{10,... | collective-permute-start | bytes 835592 | tf_op jit(solution)/shard_map/ppermute | solution.py:20
  140.3 6.9 %collective-permute-start.22 = (bf16[64,512]{1,0:T(8,128)(2,1)S(1)}, bf16[64,512]{1,0:T(8,128)(2,1)S(1)}, u32[]{:S(2)}, u32[]{:S(2)}) collective-permute-start(bf16[64,512]{1,0:T(8,128)(2,1)S(1)} %get-tuple-element.26), channel_id=1, source_target_pairs={{0,12},{4,8},{8,4},{12,0},{1,13},{5,9},{9,5},{13,1},{2,14},{6,10},... | collective-permute-start | bytes 196616 | tf_op jit(solution)/shard_map/ppermute | solution.py:20
  142.4 7.5 %collective-permute-start.23 = (bf16[64,512]{1,0:T(8,128)(2,1)S(1)}, bf16[64,512]{1,0:T(8,128)(2,1)S(1)}, u32[]{:S(2)}, u32[]{:S(2)}) collective-permute-start(bf16[64,512]{1,0:T(8,128)(2,1)S(1)} %get-tuple-element.28), channel_id=1, source_target_pairs={{0,8},{4,12},{8,0},{12,4},{1,9},{5,13},{9,1},{13,5},{2,10},{6,14},... | collective-permute-start | bytes 196616 | tf_op jit(solution)/shard_map/ppermute | solution.py:20
  143.2 6.6 %collective-permute-start.24 = (bf16[64,512]{1,0:T(8,128)(2,1)S(1)}, bf16[64,512]{1,0:T(8,128)(2,1)S(1)}, u32[]{:S(2)}, u32[]{:S(2)}) collective-permute-start(bf16[64,512]{1,0:T(8,128)(2,1)S(1)} %get-tuple-element.27), channel_id=1, source_target_pairs={{0,4},{4,0},{8,12},{12,8},{1,5},{5,1},{9,13},{13,9},{2,6},{6,2},{1... | collective-permute-start | bytes 196616 | tf_op jit(solution)/shard_map/ppermute | solution.py:20
  (12 other events, 254.7 us)

commit v2 on v1

--- a/solution.py
+++ b/solution.py
@@ -1,6 +1,10 @@
+import functools
+
 import jax
 import jax.numpy as jnp
 from jax import lax
+from jax.experimental import pallas as pl
+from jax.experimental.pallas import tpu as pltpu
 from jax.sharding import PartitionSpec as P
 
 WIDTH = 8192
@@ -201,7 +205,342 @@
     return (hidden_out, new_state, window[:, 1:], group_window[:, 1:])
 
 
+IN_VMEM = pl.BlockSpec(memory_space=pltpu.VMEM)
+IN_PLACE = pl.BlockSpec(memory_space=pl.ANY)
+IN_SMEM = pl.BlockSpec(memory_space=pltpu.SMEM)
+MIB = 1 << 20
+
+
+def cost_of(reads, flops):
+    return pl.CostEstimate(flops=flops, bytes_accessed=reads, transcendentals=0)
+
+
+def call(body, name, places, arrays, outs, flops, weight=None, scratch=(), room=8 * MIB):
+    given = [*arrays] if weight is None else [*arrays, weight]
+    reads = sum(a.size * a.dtype.itemsize for a in given)
+    return pl.pallas_call(
+        body,
+        in_specs=[IN_SMEM] + [IN_VMEM] * len(arrays) + [IN_PLACE] * (weight is not None),
+        out_specs=[IN_VMEM] * len(outs),
+        out_shape=[jax.ShapeDtypeStruct(shape, dtype) for shape, dtype in outs],
+        scratch_shapes=list(scratch),
+        compiler_params=pltpu.CompilerParams(vmem_limit_bytes=room),
+        cost_estimate=cost_of(reads, flops),
+        name=name,
+    )(jnp.stack(places).astype(jnp.int32), *given)
+
+
+def started(copies):
+    copies = [pltpu.make_async_copy(*copy) for copy in copies]
+    for copy in copies:
+        copy.start()
+    return copies
+
+
+def fetch_body(pieces, source, target, semaphores):
+    step = source.shape[0] // pieces
+    copies = [
+        pltpu.make_async_copy(source.at[pl.ds(i * step, step)], target.at[pl.ds(i * step, step)], semaphores.at[i])
+        for i in range(pieces)
+    ]
+    for copy in copies:
+        copy.start()
+    for copy in copies:
+        copy.wait()
+
+
+def fetched(weight, after, name, pieces=8):
+    weight, _ = lax.optimization_barrier((weight, after))
+    return pl.pallas_call(
+        functools.partial(fetch_body, pieces),
+        in_specs=[pl.BlockSpec(memory_space=pl.ANY)],
+        out_specs=IN_VMEM,
+        out_shape=jax.ShapeDtypeStruct(weight.shape, weight.dtype),
+        scratch_shapes=[pltpu.SemaphoreType.DMA((pieces,))],
+        compiler_params=pltpu.CompilerParams(vmem_limit_bytes=(34 if weight.size > 6 * MIB else 40) * MIB),
+        cost_estimate=cost_of(2 * weight.size * weight.dtype.itemsize, 0),
+        name=name,
+    )(weight)
+
+
+def two_columns(square):
+    high, low = split_pair(square)
+    lanes = lax.broadcasted_iota(jnp.int32, (square.shape[0], 128), 1)
+    return jnp.where(lanes == 0, high.astype(f32), jnp.where(lanes == 1, low.astype(f32), 0.0)).astype(bf16)
+
+
+def from_two(tail):
+    return jnp.sum(tail[:, :2].astype(f32), axis=1, keepdims=True)
+
+
+def spread_body(own, wide, heads, place, *refs):
+    count = len(refs) - 4
+    blocks, group_w, step_w, small, spread = refs[:count], refs[-4], refs[-3], refs[-2], refs[-1]
+    rows = small.shape[0]
+    index = place[0]
+    groups = jnp.zeros((rows, wide), f32)
+    steps = jnp.zeros((rows, heads), f32)
+    square = jnp.zeros((rows, 1), f32)
+    piece = 256
+    unit = lax.broadcasted_iota(jnp.int32, (piece, 2 * piece), 0) * 2
+    target = lax.broadcasted_iota(jnp.int32, (piece, 2 * piece), 1)
+    for k in range(count):
+        block = blocks[k][:, :own]
+        start = pl.multiple_of((index ^ k) * own, own)
+        groups += jnp.dot(block, group_w[pl.ds(start, own), :], preferred_element_type=f32)
+        steps += lax.dot_general(
+            block, step_w[:, pl.ds(start, own)], (((1,), (1,)), ((), ())), preferred_element_type=f32
+        )
+        square += from_two(blocks[k][:, own:])
+    small[:, :wide] = groups
+    lanes = lax.broadcasted_iota(jnp.int32, (rows, 128), 1)
+    small[:, wide:] = jnp.where(lanes == 127, square, 0.0)
+    small[:, wide : wide + heads] = steps
+    for which in range(2):
+        ones = (unit + which == target).astype(bf16)
+        for k in range(count):
+            for j in range(own // piece):
+                part = jnp.dot(blocks[k][:, j * piece : (j + 1) * piece], ones, preferred_element_type=f32)
+                spread[k, which * rows : (which + 1) * rows, 2 * j * piece : 2 * (j + 1) * piece] = part.astype(bf16)
+
+
+def gates_body(own, width, place, spread, weight, mine, other, held, total, arrived):
+    index, chip, core = place[0], place[1], place[2]
+    count, rows = spread.shape[0], spread.shape[1] // 2
+    piece = own // 2
+    copies = started(
+        (
+            weight.at[pl.ds(pl.multiple_of((index ^ (i // 2)) * own + (i % 2) * piece, piece), piece)],
+            held.at[pl.ds(i * piece, piece)],
+            arrived.at[i],
+        )
+        for i in range(2 * count)
+    )
+    for i in range(2 * count):
+        copies[i].wait()
+        block = spread[i // 2, :, (i % 2) * 2 * piece : (i % 2 + 1) * 2 * piece]
+        for t in range(2 * mine.shape[0]):
+            side, q = divmod(t, mine.shape[0])
+            column = pl.multiple_of((((chip ^ q) * 2) + (core ^ (1 - side))) * width, width)
+            rows_of = held[i * piece : (i + 1) * piece, :, pl.ds(column, width)].reshape(2 * piece, width)
+            value = jnp.dot(block, rows_of, preferred_element_type=f32)
+            if i > 0:
+                value += total[t]
+            if i < 2 * count - 1:
+                total[t] = value
+                continue
+            to = mine if side else other
+            to[q, 0] = value[:rows].astype(to.dtype)
+            to[q, 1] = value[rows:].astype(to.dtype)
+
+
+def out_body(own, width, mean_over, count, place, *refs):
+    blocks, weight, outs = refs[:count], refs[count], refs[count + 1 :]
+    at_short, at_long = place[0], place[1]
+    square = from_two(blocks[0][:, width:])
+    for k in range(1, count):
+        square += from_two(blocks[k][:, width:])
+    scale = lax.rsqrt(square / mean_over + epsilon)
+    for q in range(len(outs) - 1, -1, -1):
+        column = pl.multiple_of((at_long ^ q) * own, own)
+        total = jnp.zeros(outs[q].shape, f32)
+        for k in range(count):
+            start = pl.multiple_of((at_short ^ k) * width, width)
+            total += jnp.dot(
+                blocks[k][:, :width], weight[pl.ds(start, width), pl.ds(column, own)], preferred_element_type=f32
+            )
+        outs[q][...] = (total * scale).astype(outs[q].dtype)
+
+
+def up_body(own, place, *refs):
+    count = len(refs) - 3
+    blocks, weight, mine, other = refs[:count], refs[-3], refs[-2], refs[-1]
+    index, core = place[0], place[1]
+    half = weight.shape[1] // 2
+    piece = 512
+    square = from_two(blocks[0][:, own:])
+    for k in range(1, count):
+        square += from_two(blocks[k][:, own:])
+    for side in range(2):
+        for j in range(half // piece):
+            column = pl.multiple_of((core ^ (1 - side)) * half + j * piece, piece)
+            total = jnp.zeros((mine.shape[0], piece), f32)
+            for k in range(count):
+                start = pl.multiple_of((index ^ k) * own, own)
+                total += jnp.dot(
+                    blocks[k][:, :own], weight[pl.ds(start, own), pl.ds(column, piece)], preferred_element_type=f32
+                )
+            if side == 0:
+                other[:, j * piece : (j + 1) * piece] = total.astype(bf16)
+            else:
+                mine[:, j * piece : (j + 1) * piece] = total
+    other[:, half:] = two_columns(square)
+    mine[:, half:] = jnp.broadcast_to(square, (square.shape[0], 128))
+
+
+def down_body(own, place, first, second, weight, *outs):
+    core, at_long = place[0], place[1]
+    half = first.shape[1]
+    for q in range(len(outs) - 1, -1, -1):
+        column = pl.multiple_of((at_long ^ q) * own, own)
+        total = jnp.zeros(outs[q].shape, f32)
+        for k, block in enumerate((first, second)):
+            start = pl.multiple_of((core ^ k) * half, half)
+            total += jnp.dot(block[...], weight[pl.ds(start, half), pl.ds(column, own)], preferred_element_type=f32)
+        outs[q][...] = total.astype(outs[q].dtype)
+
+
+def exchanged(value, axis):
+    return [value] + [swap(value, axis, k) for k in range(1, lax.axis_size(axis))]
+
+
+def fast(
+    hidden_in,
+    mixer_gain,
+    mlp_gain,
+    gate_in_weight,
+    group_weight,
+    step_weight,
+    step_bias,
+    decay_log,
+    skip_scale,
+    conv_weight,
+    group_conv_weight,
+    conv_state,
+    group_conv_state,
+    ssm_state,
+    norm_gain,
+    out_weight,
+    up_weight,
+    down_weight,
+):
+    rows, own = hidden_in.shape
+    longs, shorts = lax.axis_size("long"), lax.axis_size("short")
+    at_long, at_short = lax.axis_index("long"), lax.axis_index("short")
+    core, chip = at_short & 1, at_short // 2
+    chips = shorts // 2
+    wide, heads = group_weight.shape[1], step_weight.shape[1]
+    heads_here = heads // shorts
+    width = heads_here * HEAD_DIM
+
+    features = hidden_in.astype(f32)
+    scaled_own = (features * mixer_gain.astype(f32)).astype(bf16)
+    payload = with_square(scaled_own, jnp.sum(features * features, axis=1))
+    blocks = exchanged(payload, "long")
+    small, spread = call(
+        functools.partial(spread_body, own, wide, heads),
+        "spread",
+        [at_long],
+        [*blocks, group_weight, step_weight.T],
+        [((rows, wide + 128), f32), ((longs, 2 * rows, 2 * own), bf16)],
+        2 * rows * longs * own * (wide + heads + 1024),
+    )
+    small = total_over(small, "short")
+    inverse = lax.rsqrt(small[:, -1:] / WIDTH + epsilon)
+    group_raw = small[:, :wide] * inverse
+    step_raw = lax.dynamic_slice_in_dim(small, wide + at_short * heads_here, heads_here, 1) * inverse
+
+    mine, other = call(
+        functools.partial(gates_body, own, width),
+        "gates",
+        [at_long, chip, core],
+        [spread],
+        [((chips, 2, rows, width), f32), ((chips, 2, rows, width), bf16)],
+        2 * 128 * gate_in_weight.size,
+        gate_in_weight,
+        [
+            pltpu.VMEM(gate_in_weight.shape, bf16),
+            pltpu.VMEM((shorts, 2 * rows, width), f32),
+            pltpu.SemaphoreType.DMA((2 * longs,)),
+        ],
+        46 * MIB,
+    )
+    mine = mine + swap(other, "short", 1).astype(f32)
+    gate_in = mine[0]
+    for q in range(1, chips):
+        gate_in = gate_in + swap(mine[q].astype(bf16), "short", 2 * q).astype(f32)
+    gate_in = gate_in * inverse
+
+    group_window = jnp.concatenate([group_conv_state, group_raw[:, None, :]], axis=1)
+    group_act = jax.nn.silu(jnp.sum(group_window * group_conv_weight[None], axis=1))
+    group_index = at_long
+    group_full = gather(group_act, "long")
+    group_full = jnp.transpose(group_full, (1, 0, 2)).reshape(rows, longs * wide)
+    state_in = lax.dynamic_slice_in_dim(group_full, group_index * STATE, STATE, 1)
+    state_out = lax.dynamic_slice_in_dim(group_full, (GROUPS + group_index) * STATE, STATE, 1)
+
+    step_size = jax.nn.softplus(step_raw + step_bias[None])
+    decay = jnp.exp(-jnp.exp(decay_log)[None] * step_size)
+    window = jnp.concatenate([conv_state, gate_in[1][:, None, :]], axis=1)
+    mixer_input = jax.nn.silu(jnp.sum(window * conv_weight[None], axis=1))
+    head_input = mixer_input.reshape(rows, heads_here, HEAD_DIM)
+    new_state = (
+        decay[:, :, None, None] * ssm_state
+        + (step_size[:, :, None] * head_input)[:, :, :, None] * state_in[:, None, None, :]
+    )
+    readout = jnp.sum(new_state * state_out[:, None, None, :], axis=-1)
+    readout = readout + skip_scale[None, :, None] * head_input
+    readout = readout.reshape(rows, width) * jax.nn.silu(gate_in[0])
+
+    unscaled = (readout * norm_gain[None]).astype(bf16)
+    payload = with_square(unscaled, jnp.sum(readout * readout, axis=1))
+    mixed_weight = fetched(out_weight, payload, "fetch_mixed")
+    blocks = exchanged(payload, "short")
+    mixed = call(
+        functools.partial(out_body, own, width, INNER // GROUPS, shorts),
+        "mixed",
+        [at_short, at_long],
+        [*blocks, mixed_weight],
+        [((rows, own), f32)] + [((rows, own), bf16)] * (longs - 1),
+        2 * rows * out_weight.size,
+    )
+    total = features + mixed[0]
+    for k in range(longs - 1, 0, -1):
+        total = total + swap(mixed[k], "long", k).astype(f32)
+    middle = total.astype(bf16).astype(f32)
+
+    scaled_own = (middle * mlp_gain.astype(f32)).astype(bf16)
+    payload = with_square(scaled_own, jnp.sum(middle * middle, axis=1))
+    upward_weight = fetched(up_weight, payload, "fetch_upward")
+    blocks = exchanged(payload, "long")
+    half = up_weight.shape[1] // 2
+    mine, other = call(
+        functools.partial(up_body, own),
+        "upward",
+        [at_long, core],
+        [*blocks, upward_weight],
+        [((rows, half + 128), f32), ((rows, half + 128), bf16)],
+        2 * rows * up_weight.size,
+    )
+
+    def added(to, arrived):
+        square = to[:, half:] + square_of(arrived[:, half:])[:, None]
+        return jnp.concatenate([to[:, :half] + arrived[:, :half].astype(f32), square], axis=1)
+
+    upward = added(mine, swap(other, "short", 1))
+    sent = with_square(upward[:, :half].astype(bf16), upward[:, half])
+    downward_weight = fetched(down_weight, sent, "fetch_downward")
+    for k in range(1, chips):
+        arrived, downward_weight = lax.optimization_barrier((swap(sent, "short", 2 * k), downward_weight))
+        upward = added(upward, arrived)
+    inverse_mid = lax.rsqrt(upward[:, half:][:, :1] / WIDTH + epsilon)
+    active = jnp.square(jnp.maximum(upward[:, :half] * inverse_mid, 0.0)).astype(bf16)
+    parts = call(
+        functools.partial(down_body, own),
+        "downward",
+        [core, at_long],
+        [active, swap(active, "short", 1), downward_weight],
+        [((rows, own), f32)] + [((rows, own), bf16)] * (longs - 1),
+        2 * rows * down_weight.size,
+    )
+    total = middle + parts[0]
+    for k in range(longs - 1, 0, -1):
+        total = total + swap(parts[k], "long", k).astype(f32)
+    return (total.astype(bf16), new_state, window[:, 1:], group_window[:, 1:])
+
+
 def solution(mesh):
+    whole_groups = mesh.shape["long"] == GROUPS and mesh.shape["short"] == 4
     placed = (
         P("groups", ("short", "long")),
         P(("short", "long")),
@@ -223,7 +562,7 @@
         P("long", "short"),
     )
     return jax.shard_map(
-        local,
+        fast if whole_groups else local,
         mesh=mesh,
         in_specs=placed,
         out_specs=(

time: 151 us -> 114 us (0.75)
  matrix products: 39.3 us -> 0 us
  Pallas kernels: 0 us -> 32.7 us
  waiting for transfers between devices: 44.4 us -> 24.3 us
  local copies, waits for them, and re-layouts: 8.82 us -> 4.87 us
  other arithmetic: 25.7 us -> 22.2 us
  starting transfers between devices: 30.9 us -> 28.6 us
    dot_general x6 -> x0, matrix products: 39.3 us -> none  [the longest x1 15.2 us: local(): jnp.einsum('rd,dkc->krc', scaled, gate_in_weight, preferred_element_type=...]
    pallas_call x0 -> x8, Pallas kernels: none -> 32.7 us  [the longest x5 17.4 us: call(): pl.pallas_call(body, in_specs=[IN_SMEM] + [IN_VMEM] * len(arrays) + [IN_P...]
    ppermute x25, waiting for transfers between devices: 44.4 us -> 24.3 us  [swap(): return lax.ppermute(value, axis, [(i, i ^ bits) for i in range(size)])]
    reshape x7 -> x0, local copies, waits for them, and re-layouts: 2.47 us -> none  [the longest x1 0.81 us: chip_scatter_sum(): parts = parts.reshape((size // 2, 2) + parts.shape[1:])]
    ppermute x25, starting transfers between devices: 30.9 us -> 28.6 us  [swap(): return lax.ppermute(value, axis, [(i, i ^ bits) for i in range(size)])]
    reduce_sum x8 -> x5, other arithmetic: 16.6 us -> 14.7 us  [the longest x1 14.4 us: fast(): readout = jnp.sum(new_state * state_out[:, None, None, :], axis=-1)]
  transfers between devices with their start and end apart: 25 -> 25, of which waited for: 17 -> 11; matrix products, arithmetic and copies ran while one was open for 16% -> 5% of each run, Pallas kernels for 0% -> 20%
where the time goes in v2:
time: 114 us
  Pallas kernels  32.7 us (29%)
  starting transfers between devices  28.6 us (25%)
  waiting for transfers between devices  24.3 us (21%)
  other arithmetic  22.2 us (19%)
  local copies, waits for them, and re-layouts  4.87 us (4%)
  between operations  1.22 us (1%)
    ppermute x25, starting transfers between devices, swap(): return lax.ppermute(value, axis, [(i, i ^ bits) for i in range(size)])  28.6 us
    ppermute x25, waiting for transfers between devices, swap(): return lax.ppermute(value, axis, [(i, i ^ bits) for i in range(size)])  24.3 us
    pallas_call x5, Pallas kernels, call(): pl.pallas_call(body, in_specs=[IN_SMEM] + [IN_VMEM] * len(arrays) + [IN_P...  17.4 us
    pallas_call x3, Pallas kernels, fetched(): pl.pallas_call(functools.partial(fetch_body, pieces), in_specs=[pl.BlockS...  15.3 us
    reduce_sum x1, other arithmetic, fast(): readout = jnp.sum(new_state * state_out[:, None, None, :], axis=-1)  14.4 us
  transfers between devices with their start and end apart: 25, of which 11 were waited for; matrix products, arithmetic and copies ran while one was open for 5% of the time, Pallas kernels for 20%

profile of v2, /device:TPU:0, one launch (start us, length us, event | category | flops | bytes accessed | tf_op | source)
XLA Modules:
  0.0 114.0 jit_solution(15397912060197909151)
XLA Ops:
  2.5 3.1 %collective-permute-start = (bf16[64,640]{1,0:T(8,128)(2,1)S(1)}, bf16[64,640]{1,0:T(8,128)(2,1)S(1)}, u32[]{:S(2)}, u32[]{:S(2)}) collective-permute-start(bf16[64,640]{1,0:T(8,128)(2,1)S(1)} %pad_maximum_fusion.4.refs_0_), channel_id=1, source_target_pairs={{0,4},{4,0},{8,12},{12,8},{1,5},{5,1},{9,13},{13,9},{2,6},{6,2},{1... | collective-permute-start | bytes 245768 | tf_op jit(solution)/shard_map/ppermute | solution.py:24
  5.6 2.6 %collective-permute-start.1 = (bf16[64,640]{1,0:T(8,128)(2,1)S(1)}, bf16[64,640]{1,0:T(8,128)(2,1)S(1)}, u32[]{:S(2)}, u32[]{:S(2)}) collective-permute-start(bf16[64,640]{1,0:T(8,128)(2,1)S(1)} %pad_maximum_fusion.4.refs_0_), channel_id=1, source_target_pairs={{0,8},{4,12},{8,0},{12,4},{1,9},{5,13},{9,1},{13,5},{2,10},{6,14},... | collective-permute-start | bytes 245768 | tf_op jit(solution)/shard_map/ppermute | solution.py:24
  9.7 5.1 %collective-permute-done.1.refs_2_ = bf16[64,640]{1,0:T(8,128)(2,1)S(1)} collective-permute-done((bf16[64,640]{1,0:T(8,128)(2,1)S(1)}, bf16[64,640]{1,0:T(8,128)(2,1)S(1)}, u32[]{:S(2)}, u32[]{:S(2)}) %collective-permute-start.1) | collective-permute-done | bytes 81952 | tf_op jit(solution)/shard_map/ppermute | solution.py:24
  19.4 1.6 %collective-permute-start.4 = (f32[64,384]{1,0:T(8,128)S(1)}, f32[64,384]{1,0:T(8,128)S(1)}, u32[]{:S(2)}, u32[]{:S(2)}) collective-permute-start(f32[64,384]{1,0:T(8,128)S(1)} %add.147), channel_id=1, source_target_pairs={{0,2},{1,3},{2,0},{3,1},{4,6},{5,7},{6,4},{7,5},{8,10},{9,11},{10,... | collective-permute-start | bytes 294920 | tf_op jit(solution)/shard_map/ppermute | solution.py:24
  21.0 7.0 %gates.1 = (f32[2,2,64,512]{3,2,1,0:T(8,128)S(1)}, bf16[2,2,64,512]{3,2,1,0:T(8,128)(2,1)S(1)}) custom-call(s32[3]{0:T(128)S(1)} %pad_add_fusion.1.place, bf16[4,128,1024]{2,1,0:T(8,128)(2,1)S(1)} %get-tuple-element.24.spread, bf16[2048,2,2048]{2,1,0:T(2,128)(2,1)} %weight.1), custom_call_target="tpu_custom_call" | custom-call | flops 2147483648 | bytes 17825792 | tf_op jit(solution)/shard_map/gates/pallas_call | solution.py:221
  28.4 2.5 %collective-permute-start.9 = (f32[64,256]{1,0:T(8,128)S(1)}, f32[64,256]{1,0:T(8,128)S(1)}, u32[]{:S(2)}, u32[]{:S(2)}) collective-permute-start(f32[64,256]{1,0:T(8,128)S(1)} %divide_multiply_fusion), channel_id=1, source_target_pairs={{0,12},{4,8},{8,4},{12,0},{1,13},{5,9},{9,5},{13,1},{2,14},{6,10},... | collective-permute-start | bytes 196616 | tf_op jit(solution)/shard_map/ppermute | solution.py:24
  33.8 4.2 %collective-permute-done.8 = f32[64,256]{1,0:T(8,128)S(1)} collective-permute-done((f32[64,256]{1,0:T(8,128)S(1)}, f32[64,256]{1,0:T(8,128)S(1)}, u32[]{:S(2)}, u32[]{:S(2)}) %collective-permute-start.8) | collective-permute-done | bytes 65568 | tf_op jit(solution)/shard_map/ppermute | solution.py:24
  40.7 14.4 %multiply_reduce_fusion = (f32[64,8,64]{2,1,0:T(8,128)S(1)}, f32[64,8,64,128]{3,2,1,0:T(8,128)}) fusion(f32[64,128]{1,0:T(8,128)S(1)} %get-tuple-element.53, f32[64,128]{1,0:T(8,128)S(1)} %get-tuple-element.52, f32[64,8,64]{2,1,0:T(8,128)S(1)} %multiply_multiply_fusion, f32[64,8,64,128]{3,2,1,0:T(8,128)} %param.31, f32[64,8]{1,0:T(8,128)S(1)} %get-tuple-element.50), kind=kLoop, calls=%fused_computation | loop fusion | flops 20938752 | bytes 33884160 | tf_op jit(solution)/shard_map/reduce_sum | solution.py:481
  57.6 3.5 %fetch_mixed.1.refs_4_ = bf16[2048,2048]{1,0:T(8,128)(2,1)S(1)} custom-call(bf16[2048,2048]{1,0:T(8,128)(2,1)} %source), custom_call_target="tpu_custom_call" | custom-call | bytes 16777216 | tf_op jit(solution)/shard_map/fetch_mixed/pallas_call | solution.py:254
  61.8 2.1 %mixed.1 = (f32[64,512]{1,0:T(8,128)S(1)}, bf16[64,512]{1,0:T(8,128)(2,1)S(1)}, bf16[64,512]{1,0:T(8,128)(2,1)S(1)}, bf16[64,512]{1,0:T(8,128)(2,1)S(1)}) custom-call(s32[2]{0:T(128)S(1)} %pad_add_fusion.place, bf16[64,640]{1,0:T(8,128)(2,1)S(1)} %pad_maximum_fusion.5.refs_0_, bf16[64,640]{1,0:T(8,128)(2,1)S(1)} %collective-permute-done.10.refs_1_, ...), custom_call_target="tpu_custom_call" | custom-call | flops 536870912 | bytes 8716288 | tf_op jit(solution)/shard_map/mixed/pallas_call | solution.py:221
  64.1 2.9 %collective-permute-start.14 = (bf16[64,512]{1,0:T(8,128)(2,1)S(1)}, bf16[64,512]{1,0:T(8,128)(2,1)S(1)}, u32[]{:S(2)}, u32[]{:S(2)}) collective-permute-start(bf16[64,512]{1,0:T(8,128)(2,1)S(1)} %get-tuple-element.30), channel_id=1, source_target_pairs={{0,8},{4,12},{8,0},{12,4},{1,9},{5,13},{9,1},{13,5},{2,10},{6,14},... | collective-permute-start | bytes 196616 | tf_op jit(solution)/shard_map/ppermute | solution.py:24
  69.4 1.7 %collective-permute-done.14 = bf16[64,512]{1,0:T(8,128)(2,1)S(1)} collective-permute-done((bf16[64,512]{1,0:T(8,128)(2,1)S(1)}, bf16[64,512]{1,0:T(8,128)(2,1)S(1)}, u32[]{:S(2)}, u32[]{:S(2)}) %collective-permute-start.14) | collective-permute-done | bytes 65568 | tf_op jit(solution)/shard_map/ppermute | solution.py:24
  71.1 2.1 %collective-permute-done.13 = bf16[64,512]{1,0:T(8,128)(2,1)S(1)} collective-permute-done((bf16[64,512]{1,0:T(8,128)(2,1)S(1)}, bf16[64,512]{1,0:T(8,128)(2,1)S(1)}, u32[]{:S(2)}, u32[]{:S(2)}) %collective-permute-start.13) | collective-permute-done | bytes 65568 | tf_op jit(solution)/shard_map/ppermute | solution.py:24
  74.5 1.6 %collective-permute-start.17 = (bf16[64,640]{1,0:T(8,128)(2,1)S(1)}, bf16[64,640]{1,0:T(8,128)(2,1)S(1)}, u32[]{:S(2)}, u32[]{:S(2)}) collective-permute-start(bf16[64,640]{1,0:T(8,128)(2,1)S(1)} %pad_maximum_fusion.6.refs_0_), channel_id=1, source_target_pairs={{0,8},{4,12},{8,0},{12,4},{1,9},{5,13},{9,1},{13,5},{2,10},{6,14},... | collective-permute-start | bytes 245768 | tf_op jit(solution)/shard_map/ppermute | solution.py:24
  76.1 1.8 %collective-permute-start.18 = (bf16[64,640]{1,0:T(8,128)(2,1)S(1)}, bf16[64,640]{1,0:T(8,128)(2,1)S(1)}, u32[]{:S(2)}, u32[]{:S(2)}) collective-permute-start(bf16[64,640]{1,0:T(8,128)(2,1)S(1)} %pad_maximum_fusion.6.refs_0_), channel_id=1, source_target_pairs={{0,12},{4,8},{8,4},{12,0},{1,13},{5,9},{9,5},{13,1},{2,14},{6,10},... | collective-permute-start | bytes 245768 | tf_op jit(solution)/shard_map/ppermute | solution.py:24
  78.0 5.9 %fetch_upward.1.refs_4_ = bf16[2048,4096]{1,0:T(8,128)(2,1)S(1)} custom-call(bf16[2048,4096]{1,0:T(8,128)(2,1)} %source.1), custom_call_target="tpu_custom_call" | custom-call | bytes 33554432 | tf_op jit(solution)/shard_map/fetch_upward/pallas_call | solution.py:254
  84.0 3.6 %upward.1 = (f32[64,2176]{1,0:T(8,128)S(1)}, bf16[64,2176]{1,0:T(8,128)(2,1)S(1)}) custom-call(s32[2]{0:T(128)S(1)} %pad_add_fusion.3.place, bf16[64,640]{1,0:T(8,128)(2,1)S(1)} %pad_maximum_fusion.6.refs_0_, bf16[64,640]{1,0:T(8,128)(2,1)S(1)} %collective-permute-done.16.refs_1_, bf16[64,640]{1,0:T(8,128)(2,1)S(1)} %collective-permute-done.17.refs_2_, ...), custom_call_target="tpu_custom_call" | custom-call | flops 1073741824 | bytes 17104896 | tf_op jit(solution)/shard_map/upward/pallas_call | solution.py:221
  87.7 1.5 %collective-permute-done.19 = bf16[64,2176]{1,0:T(8,128)(2,1)S(1)} collective-permute-done((bf16[64,2176]{1,0:T(8,128)(2,1)S(1)}, bf16[64,2176]{1,0:T(8,128)(2,1)S(1)}, u32[]{:S(2)}, u32[]{:S(2)}) %collective-permute-start.19) | collective-permute-done | bytes 278560 | tf_op jit(solution)/shard_map/ppermute | solution.py:24
  90.5 5.9 %fetch_downward.1.weight = bf16[4096,2048]{1,0:T(8,128)(2,1)S(1)} custom-call(bf16[4096,2048]{1,0:T(8,128)(2,1)} %source.2), custom_call_target="tpu_custom_call" | custom-call | bytes 33554432 | tf_op jit(solution)/shard_map/fetch_downward/pallas_call | solution.py:254
  96.4 2.1 %collective-permute-done.20 = bf16[64,2176]{1,0:T(8,128)(2,1)S(1)} collective-permute-done((bf16[64,2176]{1,0:T(8,128)(2,1)S(1)}, bf16[64,2176]{1,0:T(8,128)(2,1)S(1)}, u32[]{:S(2)}, u32[]{:S(2)}) %collective-permute-start.20) | collective-permute-done | bytes 278560 | tf_op jit(solution)/shard_map/ppermute | solution.py:24
  100.7 3.6 %downward.1 = (f32[64,512]{1,0:T(8,128)S(1)}, bf16[64,512]{1,0:T(8,128)(2,1)S(1)}, bf16[64,512]{1,0:T(8,128)(2,1)S(1)}, bf16[64,512]{1,0:T(8,128)(2,1)S(1)}) custom-call(s32[2]{0:T(128)S(1)} %pad_add_fusion.2.place, bf16[64,2048]{1,0:T(8,128)(2,1)S(1)} %multiply_convert_fusion.first, bf16[64,2048]{1,0:T(8,128)(2,1)S(1)} %collective-permute-done.21.second, ...), custom_call_target="tpu_custom_call" | custom-call | flops 1073741824 | bytes 17301504 | tf_op jit(solution)/shard_map/downward/pallas_call | solution.py:221
  104.8 2.1 %collective-permute-start.23 = (bf16[64,512]{1,0:T(8,128)(2,1)S(1)}, bf16[64,512]{1,0:T(8,128)(2,1)S(1)}, u32[]{:S(2)}, u32[]{:S(2)}) collective-permute-start(bf16[64,512]{1,0:T(8,128)(2,1)S(1)} %get-tuple-element.40), channel_id=1, source_target_pairs={{0,8},{4,12},{8,0},{12,4},{1,9},{5,13},{9,1},{13,5},{2,10},{6,14},... | collective-permute-start | bytes 196616 | tf_op jit(solution)/shard_map/ppermute | solution.py:24
  106.9 1.8 %collective-permute-start.22 = (bf16[64,512]{1,0:T(8,128)(2,1)S(1)}, bf16[64,512]{1,0:T(8,128)(2,1)S(1)}, u32[]{:S(2)}, u32[]{:S(2)}) collective-permute-start(bf16[64,512]{1,0:T(8,128)(2,1)S(1)} %get-tuple-element.39), channel_id=1, source_target_pairs={{0,12},{4,8},{8,4},{12,0},{1,13},{5,9},{9,5},{13,1},{2,14},{6,10},... | collective-permute-start | bytes 196616 | tf_op jit(solution)/shard_map/ppermute | solution.py:24
  109.5 3.8 %collective-permute-done.23 = bf16[64,512]{1,0:T(8,128)(2,1)S(1)} collective-permute-done((bf16[64,512]{1,0:T(8,128)(2,1)S(1)}, bf16[64,512]{1,0:T(8,128)(2,1)S(1)}, u32[]{:S(2)}, u32[]{:S(2)}) %collective-permute-start.23) | collective-permute-done | bytes 65568 | tf_op jit(solution)/shard_map/ppermute | solution.py:24
  (119 shorter events, 26.1 us)
Async XLA Ops:
  2.5 7.2 %collective-permute-start = (bf16[64,640]{1,0:T(8,128)(2,1)S(1)}, bf16[64,640]{1,0:T(8,128)(2,1)S(1)}, u32[]{:S(2)}, u32[]{:S(2)}) collective-permute-start(bf16[64,640]{1,0:T(8,128)(2,1)S(1)} %pad_maximum_fusion.4.refs_0_), channel_id=1, source_target_pairs={{0,4},{4,0},{8,12},{12,8},{1,5},{5,1},{9,13},{13,9},{2,6},{6,2},{1... | collective-permute-start | bytes 245768 | tf_op jit(solution)/shard_map/ppermute | solution.py:24
  5.6 9.2 %collective-permute-start.1 = (bf16[64,640]{1,0:T(8,128)(2,1)S(1)}, bf16[64,640]{1,0:T(8,128)(2,1)S(1)}, u32[]{:S(2)}, u32[]{:S(2)}) collective-permute-start(bf16[64,640]{1,0:T(8,128)(2,1)S(1)} %pad_maximum_fusion.4.refs_0_), channel_id=1, source_target_pairs={{0,8},{4,12},{8,0},{12,4},{1,9},{5,13},{9,1},{13,5},{2,10},{6,14},... | collective-permute-start | bytes 245768 | tf_op jit(solution)/shard_map/ppermute | solution.py:24
  8.2 6.6 %collective-permute-start.2 = (bf16[64,640]{1,0:T(8,128)(2,1)S(1)}, bf16[64,640]{1,0:T(8,128)(2,1)S(1)}, u32[]{:S(2)}, u32[]{:S(2)}) collective-permute-start(bf16[64,640]{1,0:T(8,128)(2,1)S(1)} %pad_maximum_fusion.4.refs_0_), channel_id=1, source_target_pairs={{0,12},{4,8},{8,4},{12,0},{1,13},{5,9},{9,5},{13,1},{2,14},{6,10},... | collective-permute-start | bytes 245768 | tf_op jit(solution)/shard_map/ppermute | solution.py:24
  19.4 8.6 %collective-permute-start.4 = (f32[64,384]{1,0:T(8,128)S(1)}, f32[64,384]{1,0:T(8,128)S(1)}, u32[]{:S(2)}, u32[]{:S(2)}) collective-permute-start(f32[64,384]{1,0:T(8,128)S(1)} %add.147), channel_id=1, source_target_pairs={{0,2},{1,3},{2,0},{3,1},{4,6},{5,7},{6,4},{7,5},{8,10},{9,11},{10,... | collective-permute-start | bytes 294920 | tf_op jit(solution)/shard_map/ppermute | solution.py:24
  27.9 5.2 %collective-permute-start.5 = (bf16[2,2,64,512]{3,2,1,0:T(8,128)(2,1)S(1)}, bf16[2,2,64,512]{3,2,1,0:T(8,128)(2,1)S(1)}, u32[]{:S(2)}, u32[]{:S(2)}) collective-permute-start(bf16[2,2,64,512]{3,2,1,0:T(8,128)(2,1)S(1)} %get-tuple-element.26), channel_id=1, source_target_pairs={{0,1},{1,0},{2,3},{3,2},{4,5},{5,4},{6,7},{7,6},{8,9},{9,8},{10,11... | collective-permute-start | bytes 786440 | tf_op jit(solution)/shard_map/ppermute | solution.py:24
  28.4 9.8 %collective-permute-start.9 = (f32[64,256]{1,0:T(8,128)S(1)}, f32[64,256]{1,0:T(8,128)S(1)}, u32[]{:S(2)}, u32[]{:S(2)}) collective-permute-start(f32[64,256]{1,0:T(8,128)S(1)} %divide_multiply_fusion), channel_id=1, source_target_pairs={{0,12},{4,8},{8,4},{12,0},{1,13},{5,9},{9,5},{13,1},{2,14},{6,10},... | collective-permute-start | bytes 196616 | tf_op jit(solution)/shard_map/ppermute | solution.py:24
  30.9 7.1 %collective-permute-start.8 = (f32[64,256]{1,0:T(8,128)S(1)}, f32[64,256]{1,0:T(8,128)S(1)}, u32[]{:S(2)}, u32[]{:S(2)}) collective-permute-start(f32[64,256]{1,0:T(8,128)S(1)} %divide_multiply_fusion), channel_id=1, source_target_pairs={{0,8},{4,12},{8,0},{12,4},{1,9},{5,13},{9,1},{13,5},{2,10},{6,14},... | collective-permute-start | bytes 196616 | tf_op jit(solution)/shard_map/ppermute | solution.py:24
  31.4 6.7 %collective-permute-start.7 = (f32[64,256]{1,0:T(8,128)S(1)}, f32[64,256]{1,0:T(8,128)S(1)}, u32[]{:S(2)}, u32[]{:S(2)}) collective-permute-start(f32[64,256]{1,0:T(8,128)S(1)} %divide_multiply_fusion), channel_id=1, source_target_pairs={{0,4},{4,0},{8,12},{12,8},{1,5},{5,1},{9,13},{13,9},{2,6},{6,2},{1... | collective-permute-start | bytes 196616 | tf_op jit(solution)/shard_map/ppermute | solution.py:24
  33.2 7.0 %collective-permute-start.6 = (bf16[2,64,512]{2,1,0:T(8,128)(2,1)S(1)}, bf16[2,64,512]{2,1,0:T(8,128)(2,1)S(1)}, u32[]{:S(2)}, u32[]{:S(2)}) collective-permute-start(bf16[2,64,512]{2,1,0:T(8,128)(2,1)S(1)} %fusion.21), channel_id=1, source_target_pairs={{0,2},{1,3},{2,0},{3,1},{4,6},{5,7},{6,4},{7,5},{8,10},{9,11},{10,... | collective-permute-start | bytes 393224 | tf_op jit(solution)/shard_map/ppermute | solution.py:24
  55.5 5.5 %collective-permute-start.10 = (bf16[64,640]{1,0:T(8,128)(2,1)S(1)}, bf16[64,640]{1,0:T(8,128)(2,1)S(1)}, u32[]{:S(2)}, u32[]{:S(2)}) collective-permute-start(bf16[64,640]{1,0:T(8,128)(2,1)S(1)} %pad_maximum_fusion.5.refs_0_), channel_id=1, source_target_pairs={{0,1},{1,0},{2,3},{3,2},{4,5},{5,4},{6,7},{7,6},{8,9},{9,8},{10,11... | collective-permute-start | bytes 245768 | tf_op jit(solution)/shard_map/ppermute | solution.py:24
  55.6 5.4 %collective-permute-start.11 = (bf16[64,640]{1,0:T(8,128)(2,1)S(1)}, bf16[64,640]{1,0:T(8,128)(2,1)S(1)}, u32[]{:S(2)}, u32[]{:S(2)}) collective-permute-start(bf16[64,640]{1,0:T(8,128)(2,1)S(1)} %pad_maximum_fusion.5.refs_0_), channel_id=1, source_target_pairs={{0,2},{1,3},{2,0},{3,1},{4,6},{5,7},{6,4},{7,5},{8,10},{9,11},{10,... | collective-permute-start | bytes 245768 | tf_op jit(solution)/shard_map/ppermute | solution.py:24
  56.2 5.6 %collective-permute-start.12 = (bf16[64,640]{1,0:T(8,128)(2,1)S(1)}, bf16[64,640]{1,0:T(8,128)(2,1)S(1)}, u32[]{:S(2)}, u32[]{:S(2)}) collective-permute-start(bf16[64,640]{1,0:T(8,128)(2,1)S(1)} %pad_maximum_fusion.5.refs_0_), channel_id=1, source_target_pairs={{0,3},{1,2},{2,1},{3,0},{4,7},{5,6},{6,5},{7,4},{8,11},{9,10},{10,... | collective-permute-start | bytes 245768 | tf_op jit(solution)/shard_map/ppermute | solution.py:24
  63.9 5.5 %collective-permute-start.15 = (bf16[64,512]{1,0:T(8,128)(2,1)S(1)}, bf16[64,512]{1,0:T(8,128)(2,1)S(1)}, u32[]{:S(2)}, u32[]{:S(2)}) collective-permute-start(bf16[64,512]{1,0:T(8,128)(2,1)S(1)} %get-tuple-element.31), channel_id=1, source_target_pairs={{0,4},{4,0},{8,12},{12,8},{1,5},{5,1},{9,13},{13,9},{2,6},{6,2},{1... | collective-permute-start | bytes 196616 | tf_op jit(solution)/shard_map/ppermute | solution.py:24
  64.1 6.9 %collective-permute-start.14 = (bf16[64,512]{1,0:T(8,128)(2,1)S(1)}, bf16[64,512]{1,0:T(8,128)(2,1)S(1)}, u32[]{:S(2)}, u32[]{:S(2)}) collective-permute-start(bf16[64,512]{1,0:T(8,128)(2,1)S(1)} %get-tuple-element.30), channel_id=1, source_target_pairs={{0,8},{4,12},{8,0},{12,4},{1,9},{5,13},{9,1},{13,5},{2,10},{6,14},... | collective-permute-start | bytes 196616 | tf_op jit(solution)/shard_map/ppermute | solution.py:24
  67.0 6.2 %collective-permute-start.13 = (bf16[64,512]{1,0:T(8,128)(2,1)S(1)}, bf16[64,512]{1,0:T(8,128)(2,1)S(1)}, u32[]{:S(2)}, u32[]{:S(2)}) collective-permute-start(bf16[64,512]{1,0:T(8,128)(2,1)S(1)} %get-tuple-element.29), channel_id=1, source_target_pairs={{0,12},{4,8},{8,4},{12,0},{1,13},{5,9},{9,5},{13,1},{2,14},{6,10},... | collective-permute-start | bytes 196616 | tf_op jit(solution)/shard_map/ppermute | solution.py:24
  73.5 10.5 %collective-permute-start.16 = (bf16[64,640]{1,0:T(8,128)(2,1)S(1)}, bf16[64,640]{1,0:T(8,128)(2,1)S(1)}, u32[]{:S(2)}, u32[]{:S(2)}) collective-permute-start(bf16[64,640]{1,0:T(8,128)(2,1)S(1)} %pad_maximum_fusion.6.refs_0_), channel_id=1, source_target_pairs={{0,4},{4,0},{8,12},{12,8},{1,5},{5,1},{9,13},{13,9},{2,6},{6,2},{1... | collective-permute-start | bytes 245768 | tf_op jit(solution)/shard_map/ppermute | solution.py:24
  74.5 9.5 %collective-permute-start.17 = (bf16[64,640]{1,0:T(8,128)(2,1)S(1)}, bf16[64,640]{1,0:T(8,128)(2,1)S(1)}, u32[]{:S(2)}, u32[]{:S(2)}) collective-permute-start(bf16[64,640]{1,0:T(8,128)(2,1)S(1)} %pad_maximum_fusion.6.refs_0_), channel_id=1, source_target_pairs={{0,8},{4,12},{8,0},{12,4},{1,9},{5,13},{9,1},{13,5},{2,10},{6,14},... | collective-permute-start | bytes 245768 | tf_op jit(solution)/shard_map/ppermute | solution.py:24
  76.1 7.9 %collective-permute-start.18 = (bf16[64,640]{1,0:T(8,128)(2,1)S(1)}, bf16[64,640]{1,0:T(8,128)(2,1)S(1)}, u32[]{:S(2)}, u32[]{:S(2)}) collective-permute-start(bf16[64,640]{1,0:T(8,128)(2,1)S(1)} %pad_maximum_fusion.6.refs_0_), channel_id=1, source_target_pairs={{0,12},{4,8},{8,4},{12,0},{1,13},{5,9},{9,5},{13,1},{2,14},{6,10},... | collective-permute-start | bytes 245768 | tf_op jit(solution)/shard_map/ppermute | solution.py:24
  87.6 1.6 %collective-permute-start.19 = (bf16[64,2176]{1,0:T(8,128)(2,1)S(1)}, bf16[64,2176]{1,0:T(8,128)(2,1)S(1)}, u32[]{:S(2)}, u32[]{:S(2)}) collective-permute-start(bf16[64,2176]{1,0:T(8,128)(2,1)S(1)} %get-tuple-element.34), channel_id=1, source_target_pairs={{0,1},{1,0},{2,3},{3,2},{4,5},{5,4},{6,7},{7,6},{8,9},{9,8},{10,11... | collective-permute-start | bytes 835592 | tf_op jit(solution)/shard_map/ppermute | solution.py:24
  89.8 8.8 %collective-permute-start.20 = (bf16[64,2176]{1,0:T(8,128)(2,1)S(1)}, bf16[64,2176]{1,0:T(8,128)(2,1)S(1)}, u32[]{:S(2)}, u32[]{:S(2)}) collective-permute-start(bf16[64,2176]{1,0:T(8,128)(2,1)S(1)} %pad_maximum_fusion.2), channel_id=1, source_target_pairs={{0,2},{1,3},{2,0},{3,1},{4,6},{5,7},{6,4},{7,5},{8,10},{9,11},{10,... | collective-permute-start | bytes 835592 | tf_op jit(solution)/shard_map/ppermute | solution.py:24
  99.1 1.6 %collective-permute-start.21 = (bf16[64,2048]{1,0:T(8,128)(2,1)S(1)}, bf16[64,2048]{1,0:T(8,128)(2,1)S(1)}, u32[]{:S(2)}, u32[]{:S(2)}) collective-permute-start(bf16[64,2048]{1,0:T(8,128)(2,1)S(1)} %multiply_convert_fusion.first), channel_id=1, source_target_pairs={{0,1},{1,0},{2,3},{3,2},{4,5},{5,4},{6,7},{7,6},{8,9},{9,8},{10,11... | collective-permute-start | bytes 786440 | tf_op jit(solution)/shard_map/ppermute | solution.py:24
  104.3 5.2 %collective-permute-start.24 = (bf16[64,512]{1,0:T(8,128)(2,1)S(1)}, bf16[64,512]{1,0:T(8,128)(2,1)S(1)}, u32[]{:S(2)}, u32[]{:S(2)}) collective-permute-start(bf16[64,512]{1,0:T(8,128)(2,1)S(1)} %get-tuple-element.41), channel_id=1, source_target_pairs={{0,4},{4,0},{8,12},{12,8},{1,5},{5,1},{9,13},{13,9},{2,6},{6,2},{1... | collective-permute-start | bytes 196616 | tf_op jit(solution)/shard_map/ppermute | solution.py:24
  104.8 8.5 %collective-permute-start.23 = (bf16[64,512]{1,0:T(8,128)(2,1)S(1)}, bf16[64,512]{1,0:T(8,128)(2,1)S(1)}, u32[]{:S(2)}, u32[]{:S(2)}) collective-permute-start(bf16[64,512]{1,0:T(8,128)(2,1)S(1)} %get-tuple-element.40), channel_id=1, source_target_pairs={{0,8},{4,12},{8,0},{12,4},{1,9},{5,13},{9,1},{13,5},{2,10},{6,14},... | collective-permute-start | bytes 196616 | tf_op jit(solution)/shard_map/ppermute | solution.py:24
  106.9 6.4 %collective-permute-start.22 = (bf16[64,512]{1,0:T(8,128)(2,1)S(1)}, bf16[64,512]{1,0:T(8,128)(2,1)S(1)}, u32[]{:S(2)}, u32[]{:S(2)}) collective-permute-start(bf16[64,512]{1,0:T(8,128)(2,1)S(1)} %get-tuple-element.39), channel_id=1, source_target_pairs={{0,12},{4,8},{8,4},{12,0},{1,13},{5,9},{9,5},{13,1},{2,14},{6,10},... | collective-permute-start | bytes 196616 | tf_op jit(solution)/shard_map/ppermute | solution.py:24
  (11 other events, 200.3 us)

commit v3 on v2

--- a/solution.py
+++ b/solution.py
@@ -257,7 +257,7 @@
         out_specs=IN_VMEM,
         out_shape=jax.ShapeDtypeStruct(weight.shape, weight.dtype),
         scratch_shapes=[pltpu.SemaphoreType.DMA((pieces,))],
-        compiler_params=pltpu.CompilerParams(vmem_limit_bytes=(34 if weight.size > 6 * MIB else 40) * MIB),
+        compiler_params=pltpu.CompilerParams(vmem_limit_bytes=(34 if weight.size > 6 * MIB else 34) * MIB),
         cost_estimate=cost_of(2 * weight.size * weight.dtype.itemsize, 0),
         name=name,
     )(weight)
@@ -390,6 +390,107 @@
         outs[q][...] = total.astype(outs[q].dtype)
 
 
+def product_body(step, state, out_hi, out_lo, result, held, arrived):
+    rows, heads, size, entries = state.shape
+
+    def copy_of(i):
+        block = pl.ds(i * step, step)
+        return pltpu.make_async_copy(state.at[block], held.at[block], arrived.at[i])
+
+    for i in range(rows // step):
+        copy_of(i).start()
+
+    def one_block(i, carry):
+        copy_of(i).wait()
+        base = pl.multiple_of(i * step, step)
+        left = jnp.concatenate([out_hi[pl.ds(base, step), :], out_lo[pl.ds(base, step), :]], axis=0)
+        left = jnp.concatenate([left, left], axis=1).astype(bf16)
+        lines = []
+        for r in range(step):
+            block = held[base + r].reshape(heads * size, entries)
+            high = block.astype(bf16)
+            low = (block - high.astype(f32)).astype(bf16)
+            value = lax.dot_general(
+                left, jnp.concatenate([high, low], axis=1), (((1,), (1,)), ((), ())), preferred_element_type=f32
+            )
+            lines.append(value[r : r + 1] + value[step + r : step + r + 1])
+        result[pl.ds(base, step), :] = jnp.concatenate(lines, axis=0)
+        return carry
+
+    lax.fori_loop(0, rows // step, one_block, 0)
+
+
+def state_products(state, state_out):
+    rows, heads, size, entries = state.shape
+    step = 8
+    high, low = split_pair(state_out)
+    return pl.pallas_call(
+        functools.partial(product_body, step),
+        in_specs=[IN_PLACE, IN_VMEM, IN_VMEM],
+        out_specs=IN_VMEM,
+        out_shape=jax.ShapeDtypeStruct((rows, heads * size), f32),
+        scratch_shapes=[pltpu.VMEM(state.shape, f32), pltpu.SemaphoreType.DMA((rows // step,))],
+        compiler_params=pltpu.CompilerParams(vmem_limit_bytes=46 * MIB),
+        cost_estimate=cost_of(state.size * 4, 64 * state.size),
+        name="state_products",
+    )(state, high.astype(f32), low.astype(f32))
+
+
+def update_body(first, rows, decay, state, inputs, state_in, *refs):
+    target, held, across, arrived, sent = refs[-5:]
+    _, heads, size, _ = state.shape
+    step, together = 4, 4
+    pieces = rows // step
+    come = started(
+        (state.at[pl.ds(first + i * step, step)], held.at[pl.ds(i * step, step)], arrived.at[i]) for i in range(pieces)
+    )
+    across[...] = inputs[...].T
+    go = []
+    for i in range(pieces):
+        come[i].wait()
+
+        def some_heads(g, carry, i=i):
+            for t in range(together):
+                h = g * together + t
+                block = across[pl.ds(pl.multiple_of(h * size, size), size), first + i * step : first + (i + 1) * step]
+                for j in range(step):
+                    r = i * step + j
+                    scaled = held[r, h] * decay[(first + r) * heads + h]
+                    held[r, h] = scaled + block[:, j : j + 1] * state_in[r : r + 1, :]
+            return carry
+
+        lax.fori_loop(0, heads // together, some_heads, 0)
+        go += started([(held.at[pl.ds(i * step, step)], target.at[pl.ds(first + i * step, step)], sent.at[i])])
+    for copy in go:
+        copy.wait()
+
+
+def updated(state, decay, inputs, state_in, first, rows, before, after, name):
+    state, _ = lax.optimization_barrier((state, after))
+    given = [decay.reshape(-1), state, inputs, state_in[first : first + rows]]
+    specs = [IN_SMEM, IN_PLACE, IN_VMEM, IN_VMEM]
+    if before is not None:
+        given.append(before)
+        specs.append(IN_PLACE)
+    pieces = rows // 4
+    return pl.pallas_call(
+        functools.partial(update_body, first, rows),
+        in_specs=specs,
+        out_specs=IN_PLACE,
+        out_shape=jax.ShapeDtypeStruct(state.shape, f32),
+        scratch_shapes=[
+            pltpu.VMEM((rows,) + state.shape[1:], f32),
+            pltpu.VMEM(inputs.shape[::-1], f32),
+            pltpu.SemaphoreType.DMA((pieces,)),
+            pltpu.SemaphoreType.DMA((pieces,)),
+        ],
+        input_output_aliases={} if before is None else {4: 0},
+        compiler_params=pltpu.CompilerParams(vmem_limit_bytes=40 * MIB),
+        cost_estimate=cost_of(8 * rows * state[0].size, 3 * rows * state[0].size),
+        name=name,
+    )(*given)
+
+
 def exchanged(value, axis):
     return [value] + [swap(value, axis, k) for k in range(1, lax.axis_size(axis))]
 
@@ -431,7 +532,7 @@
         functools.partial(spread_body, own, wide, heads),
         "spread",
         [at_long],
-        [*blocks, group_weight, step_weight.T],
+        [*blocks, fetched(group_weight, payload, "fetch_groups", 2), fetched(step_weight.T, payload, "fetch_steps", 1)],
         [((rows, wide + 128), f32), ((longs, 2 * rows, 2 * own), bf16)],
         2 * rows * longs * own * (wide + heads + 1024),
     )
@@ -463,24 +564,22 @@
 
     group_window = jnp.concatenate([group_conv_state, group_raw[:, None, :]], axis=1)
     group_act = jax.nn.silu(jnp.sum(group_window * group_conv_weight[None], axis=1))
-    group_index = at_long
-    group_full = gather(group_act, "long")
-    group_full = jnp.transpose(group_full, (1, 0, 2)).reshape(rows, longs * wide)
-    state_in = lax.dynamic_slice_in_dim(group_full, group_index * STATE, STATE, 1)
-    state_out = lax.dynamic_slice_in_dim(group_full, (GROUPS + group_index) * STATE, STATE, 1)
+    low, high = group_act[:, :STATE], group_act[:, STATE:]
+    one = lax.ppermute(jnp.where(at_long < 2, high, low), "long", [(0, 1), (1, 3), (2, 0), (3, 2)])
+    two = lax.ppermute(jnp.where(at_long == 1, low, high), "long", [(1, 2), (2, 1)])
+    state_in = jnp.where(at_long == 0, low, jnp.where(at_long == 2, two, one))
+    state_out = jnp.where(at_long == 3, high, jnp.where(at_long == 1, two, one))
+    products = state_products(ssm_state, state_out)
 
     step_size = jax.nn.softplus(step_raw + step_bias[None])
     decay = jnp.exp(-jnp.exp(decay_log)[None] * step_size)
     window = jnp.concatenate([conv_state, gate_in[1][:, None, :]], axis=1)
     mixer_input = jax.nn.silu(jnp.sum(window * conv_weight[None], axis=1))
-    head_input = mixer_input.reshape(rows, heads_here, HEAD_DIM)
-    new_state = (
-        decay[:, :, None, None] * ssm_state
-        + (step_size[:, :, None] * head_input)[:, :, :, None] * state_in[:, None, None, :]
-    )
-    readout = jnp.sum(new_state * state_out[:, None, None, :], axis=-1)
-    readout = readout + skip_scale[None, :, None] * head_input
-    readout = readout.reshape(rows, width) * jax.nn.silu(gate_in[0])
+    inputs = jnp.repeat(step_size, HEAD_DIM, axis=1) * mixer_input
+    readout = jnp.repeat(decay, HEAD_DIM, axis=1) * products
+    readout = readout + inputs * jnp.sum(state_in * state_out, axis=1, keepdims=True)
+    readout = readout + jnp.repeat(skip_scale, HEAD_DIM)[None] * mixer_input
+    readout = readout * jax.nn.silu(gate_in[0])
 
     unscaled = (readout * norm_gain[None]).astype(bf16)
     payload = with_square(unscaled, jnp.sum(readout * readout, axis=1))
@@ -494,9 +593,13 @@
         [((rows, own), f32)] + [((rows, own), bf16)] * (longs - 1),
         2 * rows * out_weight.size,
     )
+    half_rows = rows // 2
+    new_state = updated(ssm_state, decay, inputs, state_in, 0, half_rows, None, mixed[-1], "update_first")
+    arrived = [swap(mixed[k], "long", k) for k in range(longs - 1, 0, -1)]
+    *arrived, new_state = lax.optimization_barrier((*arrived, new_state))
     total = features + mixed[0]
-    for k in range(longs - 1, 0, -1):
-        total = total + swap(mixed[k], "long", k).astype(f32)
+    for block in arrived:
+        total = total + block.astype(f32)
     middle = total.astype(bf16).astype(f32)
 
     scaled_own = (middle * mlp_gain.astype(f32)).astype(bf16)
@@ -533,9 +636,12 @@
         [((rows, own), f32)] + [((rows, own), bf16)] * (longs - 1),
         2 * rows * down_weight.size,
     )
+    new_state = updated(ssm_state, decay, inputs, state_in, half_rows, rows - half_rows, new_state, parts[-1], "update_last")
+    arrived = [swap(parts[k], "long", k) for k in range(longs - 1, 0, -1)]
+    *arrived, new_state = lax.optimization_barrier((*arrived, new_state))
     total = middle + parts[0]
-    for k in range(longs - 1, 0, -1):
-        total = total + swap(parts[k], "long", k).astype(f32)
+    for block in arrived:
+        total = total + block.astype(f32)
     return (total.astype(bf16), new_state, window[:, 1:], group_window[:, 1:])
 
 

time: 114 us -> 107 us (0.939)
  Pallas kernels: 32.7 us -> 52 us
  waiting for transfers between devices: 24.3 us -> 8.86 us
  other arithmetic: 22.2 us -> 8.04 us
  local copies, waits for them, and re-layouts: 4.87 us -> 6.94 us
  starting transfers between devices: 28.6 us -> 29.8 us
    pallas_call x0 -> x3, Pallas kernels: none -> 21.9 us  [the longest x2 14.9 us: updated(): pl.pallas_call(functools.partial(update_body, first, rows), in_specs=spec...]
    ppermute x25 -> x22, waiting for transfers between devices: 24.3 us -> 7.22 us  [swap(): return lax.ppermute(value, axis, [(i, i ^ bits) for i in range(size)])]
    reduce_sum x1, other arithmetic: 14.4 us -> 0.11 us  [fast(): jnp.sum(state_in * state_out, axis=1, keepdims=True)]
    ppermute x0 -> x2, starting transfers between devices: none -> 4.98 us  [the longest x1 4.32 us: fast(): lax.ppermute(jnp.where(at_long < 2, high, low), 'long', [(0, 1), (1, 3),...]
    ppermute x25 -> x22, starting transfers between devices: 28.6 us -> 24.8 us  [swap(): return lax.ppermute(value, axis, [(i, i ^ bits) for i in range(size)])]
    unnamed x21 -> x20, local copies, waits for them, and re-layouts: 2.21 us -> 5.53 us
    pallas_call x3 -> x5, Pallas kernels: 15.3 us -> 12.7 us  [fetched(): pl.pallas_call(functools.partial(fetch_body, pieces), in_specs=[pl.BlockS...]
    ppermute x0 -> x2, waiting for transfers between devices: none -> 1.64 us  [the longest x1 1.64 us: fast(): lax.ppermute(jnp.where(at_long < 2, high, low), 'long', [(0, 1), (1, 3),...]
  transfers between devices with their start and end apart: 25 -> 24, of which waited for: 11 -> 7; matrix products, arithmetic and copies ran while one was open for 5% -> 5% of each run, Pallas kernels for 20% -> 39%
where the time goes in v3:
time: 107 us
  Pallas kernels  52 us (49%)
  starting transfers between devices  29.8 us (28%)
  waiting for transfers between devices  8.86 us (8%)
  other arithmetic  8.04 us (8%)
  local copies, waits for them, and re-layouts  6.94 us (6%)
  between operations  1.23 us (1%)
    ppermute x22, starting transfers between devices, swap(): return lax.ppermute(value, axis, [(i, i ^ bits) for i in range(size)])  24.8 us
    pallas_call x5, Pallas kernels, call(): pl.pallas_call(body, in_specs=[IN_SMEM] + [IN_VMEM] * len(arrays) + [IN_P...  17.4 us
    pallas_call x2, Pallas kernels, updated(): pl.pallas_call(functools.partial(update_body, first, rows), in_specs=spec...  14.9 us
    pallas_call x5, Pallas kernels, fetched(): pl.pallas_call(functools.partial(fetch_body, pieces), in_specs=[pl.BlockS...  12.7 us
    ppermute x22, waiting for transfers between devices, swap(): return lax.ppermute(value, axis, [(i, i ^ bits) for i in range(size)])  7.22 us
    pallas_call x1, Pallas kernels, state_products(): pl.pallas_call(functools.partial(product_body, step), in_specs=[IN_PLACE,...  7 us
    unnamed x20, local copies, waits for them, and re-layouts  5.53 us
    ppermute x1, starting transfers between devices, fast(): lax.ppermute(jnp.where(at_long < 2, high, low), 'long', [(0, 1), (1, 3),...  4.32 us
  transfers between devices with their start and end apart: 24, of which 7 were waited for; matrix products, arithmetic and copies ran while one was open for 5% of the time, Pallas kernels for 39%

profile of v3, /device:TPU:0, one launch (start us, length us, event | category | flops | bytes accessed | tf_op | source)
XLA Modules:
  0.0 106.9 jit_solution(4496739281227348137)
XLA Ops:
  2.5 3.1 %collective-permute-start = (bf16[64,640]{1,0:T(8,128)(2,1)S(1)}, bf16[64,640]{1,0:T(8,128)(2,1)S(1)}, u32[]{:S(2)}, u32[]{:S(2)}) collective-permute-start(bf16[64,640]{1,0:T(8,128)(2,1)S(1)} %pad_maximum_fusion.3.refs_0_), channel_id=1, source_target_pairs={{0,4},{4,0},{8,12},{12,8},{1,5},{5,1},{9,13},{13,9},{2,6},{6,2},{1... | collective-permute-start | bytes 245768 | tf_op jit(solution)/shard_map/ppermute | solution.py:24
  5.6 2.6 %collective-permute-start.1 = (bf16[64,640]{1,0:T(8,128)(2,1)S(1)}, bf16[64,640]{1,0:T(8,128)(2,1)S(1)}, u32[]{:S(2)}, u32[]{:S(2)}) collective-permute-start(bf16[64,640]{1,0:T(8,128)(2,1)S(1)} %pad_maximum_fusion.3.refs_0_), channel_id=1, source_target_pairs={{0,8},{4,12},{8,0},{12,4},{1,9},{5,13},{9,1},{13,5},{2,10},{6,14},... | collective-permute-start | bytes 245768 | tf_op jit(solution)/shard_map/ppermute | solution.py:24
  12.7 2.1 %collective-permute-done.1.refs_2_ = bf16[64,640]{1,0:T(8,128)(2,1)S(1)} collective-permute-done((bf16[64,640]{1,0:T(8,128)(2,1)S(1)}, bf16[64,640]{1,0:T(8,128)(2,1)S(1)}, u32[]{:S(2)}, u32[]{:S(2)}) %collective-permute-start.1) | collective-permute-done | bytes 81952 | tf_op jit(solution)/shard_map/ppermute | solution.py:24
  17.3 1.6 %collective-permute-start.4 = (f32[64,384]{1,0:T(8,128)S(1)}, f32[64,384]{1,0:T(8,128)S(1)}, u32[]{:S(2)}, u32[]{:S(2)}) collective-permute-start(f32[64,384]{1,0:T(8,128)S(1)} %add.111), channel_id=1, source_target_pairs={{0,2},{1,3},{2,0},{3,1},{4,6},{5,7},{6,4},{7,5},{8,10},{9,11},{10,... | collective-permute-start | bytes 294920 | tf_op jit(solution)/shard_map/ppermute | solution.py:24
  18.9 7.0 %gates.1 = (f32[2,2,64,512]{3,2,1,0:T(8,128)S(1)}, bf16[2,2,64,512]{3,2,1,0:T(8,128)(2,1)S(1)}) custom-call(s32[3]{0:T(128)S(1)} %pad_add_fusion.1.place, bf16[4,128,1024]{2,1,0:T(8,128)(2,1)S(1)} %get-tuple-element.38.spread, bf16[2048,2,2048]{2,1,0:T(2,128)(2,1)} %weight.1), custom_call_target="tpu_custom_call" | custom-call | flops 2147483648 | bytes 17825792 | tf_op jit(solution)/shard_map/gates/pallas_call | solution.py:221
  27.0 4.3 %collective-permute-start.6 = (f32[64,128]{1,0:T(8,128)S(1)}, f32[64,128]{1,0:T(8,128)S(1)}, u32[]{:S(2)}, u32[]{:S(2)}) collective-permute-start(f32[64,128]{1,0:T(8,128)S(1)} %get-tuple-element.78), channel_id=1, source_target_pairs={{0,4},{4,12},{8,0},{12,8},{1,5},{5,13},{9,1},{13,9},{2,6},{6,14},{... | collective-permute-start | bytes 98312 | tf_op jit(solution)/shard_map/ppermute | solution.py:568
  31.9 1.6 %collective-permute-done.6 = f32[64,128]{1,0:T(8,128)S(1)} collective-permute-done((f32[64,128]{1,0:T(8,128)S(1)}, f32[64,128]{1,0:T(8,128)S(1)}, u32[]{:S(2)}, u32[]{:S(2)}) %collective-permute-start.6) | collective-permute-done | bytes 32800 | tf_op jit(solution)/shard_map/ppermute | solution.py:568
  34.4 7.0 %state_products.1 = f32[64,512]{1,0:T(8,128)S(1)} custom-call(f32[64,8,64,128]{3,2,1,0:T(8,128)} %state.3, f32[64,128]{1,0:T(8,128)S(1)} %get-tuple-element.85.out_hi, f32[64,128]{1,0:T(8,128)S(1)} %get-tuple-element.84.out_lo), custom_call_target="tpu_custom_call" | custom-call | flops 268435456 | bytes 16777216 | tf_op jit(solution)/shard_map/state_products/pallas_call | solution.py:427
  42.1 1.6 %collective-permute-start.10 = (bf16[64,640]{1,0:T(8,128)(2,1)S(1)}, bf16[64,640]{1,0:T(8,128)(2,1)S(1)}, u32[]{:S(2)}, u32[]{:S(2)}) collective-permute-start(bf16[64,640]{1,0:T(8,128)(2,1)S(1)} %pad_maximum_fusion.4.refs_0_), channel_id=1, source_target_pairs={{0,2},{1,3},{2,0},{3,1},{4,6},{5,7},{6,4},{7,5},{8,10},{9,11},{10,... | collective-permute-start | bytes 245768 | tf_op jit(solution)/shard_map/ppermute | solution.py:24
  44.1 3.4 %copy-done = bf16[2048,2048]{1,0:T(8,128)(2,1)S(1)} copy-done((bf16[2048,2048]{1,0:T(8,128)(2,1)S(1)}, bf16[2048,2048]{1,0:T(8,128)(2,1)}, u32[]{:S(2)}) %copy-start) | copy-done | bytes 8388632
  48.4 2.1 %mixed.1 = (f32[64,512]{1,0:T(8,128)S(1)}, bf16[64,512]{1,0:T(8,128)(2,1)S(1)}, bf16[64,512]{1,0:T(8,128)(2,1)S(1)}, bf16[64,512]{1,0:T(8,128)(2,1)S(1)}) custom-call(s32[2]{0:T(128)S(1)} %pad_add_fusion.place, bf16[64,640]{1,0:T(8,128)(2,1)S(1)} %pad_maximum_fusion.4.refs_0_, bf16[64,640]{1,0:T(8,128)(2,1)S(1)} %collective-permute-done.9.refs_1_, ...), custom_call_target="tpu_custom_call" | custom-call | flops 536870912 | bytes 8716288 | tf_op jit(solution)/shard_map/mixed/pallas_call | solution.py:221
  50.5 2.5 %collective-permute-start.12 = (bf16[64,512]{1,0:T(8,128)(2,1)S(1)}, bf16[64,512]{1,0:T(8,128)(2,1)S(1)}, u32[]{:S(2)}, u32[]{:S(2)}) collective-permute-start(bf16[64,512]{1,0:T(8,128)(2,1)S(1)} %get-tuple-element.43), channel_id=1, source_target_pairs={{0,12},{4,8},{8,4},{12,0},{1,13},{5,9},{9,5},{13,1},{2,14},{6,10},... | collective-permute-start | bytes 196616 | tf_op jit(solution)/shard_map/ppermute | solution.py:24
  54.9 7.4 %update_first.1.refs_0_ = f32[64,8,64,128]{3,2,1,0:T(8,128)} custom-call(f32[512]{0:T(512)S(1)} %reshape.56.decay, f32[64,8,64,128]{3,2,1,0:T(8,128)} %state.3, f32[64,512]{1,0:T(8,128)S(1)} %get-tuple-element.77.inputs, f32[32,128]{1,0:T(8,128)S(1)} %get-tuple-element.83.state_in), custom_call_target="tpu_custom_call" | custom-call | flops 6291456 | bytes 16777216 | tf_op jit(solution)/shard_map/update_first/pallas_call | solution.py:476
  63.5 2.3 %collective-permute-start.16 = (bf16[64,640]{1,0:T(8,128)(2,1)S(1)}, bf16[64,640]{1,0:T(8,128)(2,1)S(1)}, u32[]{:S(2)}, u32[]{:S(2)}) collective-permute-start(bf16[64,640]{1,0:T(8,128)(2,1)S(1)} %pad_maximum_fusion.5.refs_0_), channel_id=1, source_target_pairs={{0,8},{4,12},{8,0},{12,4},{1,9},{5,13},{9,1},{13,5},{2,10},{6,14},... | collective-permute-start | bytes 245768 | tf_op jit(solution)/shard_map/ppermute | solution.py:24
  67.3 5.9 %fetch_upward.1.refs_4_ = bf16[2048,4096]{1,0:T(8,128)(2,1)S(1)} custom-call(bf16[2048,4096]{1,0:T(8,128)(2,1)} %source.2), custom_call_target="tpu_custom_call" | custom-call | bytes 33554432 | tf_op jit(solution)/shard_map/fetch_upward/pallas_call | solution.py:254
  73.2 3.6 %upward.1 = (f32[64,2176]{1,0:T(8,128)S(1)}, bf16[64,2176]{1,0:T(8,128)(2,1)S(1)}) custom-call(s32[2]{0:T(128)S(1)} %pad_add_fusion.3.place, bf16[64,640]{1,0:T(8,128)(2,1)S(1)} %pad_maximum_fusion.5.refs_0_, bf16[64,640]{1,0:T(8,128)(2,1)S(1)} %collective-permute-done.15.refs_1_, bf16[64,640]{1,0:T(8,128)(2,1)S(1)} %collective-permute-done.16.refs_2_, ...), custom_call_target="tpu_custom_call" | custom-call | flops 1073741824 | bytes 17104896 | tf_op jit(solution)/shard_map/upward/pallas_call | solution.py:221
  76.9 1.5 %collective-permute-done.18 = bf16[64,2176]{1,0:T(8,128)(2,1)S(1)} collective-permute-done((bf16[64,2176]{1,0:T(8,128)(2,1)S(1)}, bf16[64,2176]{1,0:T(8,128)(2,1)S(1)}, u32[]{:S(2)}, u32[]{:S(2)}) %collective-permute-start.18) | collective-permute-done | bytes 278560 | tf_op jit(solution)/shard_map/ppermute | solution.py:24
  79.0 1.4 %collective-permute-start.19 = (bf16[64,2176]{1,0:T(8,128)(2,1)S(1)}, bf16[64,2176]{1,0:T(8,128)(2,1)S(1)}, u32[]{:S(2)}, u32[]{:S(2)}) collective-permute-start(bf16[64,2176]{1,0:T(8,128)(2,1)S(1)} %pad_maximum_fusion.2), channel_id=1, source_target_pairs={{0,2},{1,3},{2,0},{3,1},{4,6},{5,7},{6,4},{7,5},{8,10},{9,11},{10,... | collective-permute-start | bytes 835592 | tf_op jit(solution)/shard_map/ppermute | solution.py:24
  80.4 5.9 %fetch_downward.1.weight = bf16[4096,2048]{1,0:T(8,128)(2,1)S(1)} custom-call(bf16[4096,2048]{1,0:T(8,128)(2,1)} %source.3), custom_call_target="tpu_custom_call" | custom-call | bytes 33554432 | tf_op jit(solution)/shard_map/fetch_downward/pallas_call | solution.py:254
  86.3 1.4 %collective-permute-done.19 = bf16[64,2176]{1,0:T(8,128)(2,1)S(1)} collective-permute-done((bf16[64,2176]{1,0:T(8,128)(2,1)S(1)}, bf16[64,2176]{1,0:T(8,128)(2,1)S(1)}, u32[]{:S(2)}, u32[]{:S(2)}) %collective-permute-start.19) | collective-permute-done | bytes 278560 | tf_op jit(solution)/shard_map/ppermute | solution.py:24
  89.9 3.6 %downward.1 = (f32[64,512]{1,0:T(8,128)S(1)}, bf16[64,512]{1,0:T(8,128)(2,1)S(1)}, bf16[64,512]{1,0:T(8,128)(2,1)S(1)}, bf16[64,512]{1,0:T(8,128)(2,1)S(1)}) custom-call(s32[2]{0:T(128)S(1)} %pad_add_fusion.2.place, bf16[64,2048]{1,0:T(8,128)(2,1)S(1)} %multiply_convert_fusion.first, bf16[64,2048]{1,0:T(8,128)(2,1)S(1)} %collective-permute-done.20.second, ...), custom_call_target="tpu_custom_call" | custom-call | flops 1073741824 | bytes 17301504 | tf_op jit(solution)/shard_map/downward/pallas_call | solution.py:221
  93.5 2.5 %collective-permute-start.21 = (bf16[64,512]{1,0:T(8,128)(2,1)S(1)}, bf16[64,512]{1,0:T(8,128)(2,1)S(1)}, u32[]{:S(2)}, u32[]{:S(2)}) collective-permute-start(bf16[64,512]{1,0:T(8,128)(2,1)S(1)} %get-tuple-element.57), channel_id=1, source_target_pairs={{0,12},{4,8},{8,4},{12,0},{1,13},{5,9},{9,5},{13,1},{2,14},{6,10},... | collective-permute-start | bytes 196616 | tf_op jit(solution)/shard_map/ppermute | solution.py:24
  96.0 1.9 %collective-permute-start.23 = (bf16[64,512]{1,0:T(8,128)(2,1)S(1)}, bf16[64,512]{1,0:T(8,128)(2,1)S(1)}, u32[]{:S(2)}, u32[]{:S(2)}) collective-permute-start(bf16[64,512]{1,0:T(8,128)(2,1)S(1)} %get-tuple-element.59), channel_id=1, source_target_pairs={{0,4},{4,0},{8,12},{12,8},{1,5},{5,1},{9,13},{13,9},{2,6},{6,2},{1... | collective-permute-start | bytes 196616 | tf_op jit(solution)/shard_map/ppermute | solution.py:24
  98.7 7.4 %update_last.1 = f32[64,8,64,128]{3,2,1,0:T(8,128)} custom-call(f32[512]{0:T(512)S(1)} %reshape.56.decay, f32[64,8,64,128]{3,2,1,0:T(8,128)} %state.3, f32[64,512]{1,0:T(8,128)S(1)} %get-tuple-element.77.inputs, f32[32,128]{1,0:T(8,128)S(1)} %get-tuple-element.82.state_in, f32[64,8,64,128]{3,2,1,0:T(8,128)} %update_first.1.refs_0_), custom_call_target="tpu_custom_call", output_to_operand_aliasing={{}: (4, {})} | custom-call | flops 6291456 | bytes 16777216 | tf_op jit(solution)/shard_map/update_last/pallas_call | solution.py:476
  (114 shorter events, 21.8 us)
Async XLA Ops:
  2.5 10.2 %collective-permute-start = (bf16[64,640]{1,0:T(8,128)(2,1)S(1)}, bf16[64,640]{1,0:T(8,128)(2,1)S(1)}, u32[]{:S(2)}, u32[]{:S(2)}) collective-permute-start(bf16[64,640]{1,0:T(8,128)(2,1)S(1)} %pad_maximum_fusion.3.refs_0_), channel_id=1, source_target_pairs={{0,4},{4,0},{8,12},{12,8},{1,5},{5,1},{9,13},{13,9},{2,6},{6,2},{1... | collective-permute-start | bytes 245768 | tf_op jit(solution)/shard_map/ppermute | solution.py:24
  5.6 9.2 %collective-permute-start.1 = (bf16[64,640]{1,0:T(8,128)(2,1)S(1)}, bf16[64,640]{1,0:T(8,128)(2,1)S(1)}, u32[]{:S(2)}, u32[]{:S(2)}) collective-permute-start(bf16[64,640]{1,0:T(8,128)(2,1)S(1)} %pad_maximum_fusion.3.refs_0_), channel_id=1, source_target_pairs={{0,8},{4,12},{8,0},{12,4},{1,9},{5,13},{9,1},{13,5},{2,10},{6,14},... | collective-permute-start | bytes 245768 | tf_op jit(solution)/shard_map/ppermute | solution.py:24
  8.2 6.6 %collective-permute-start.2 = (bf16[64,640]{1,0:T(8,128)(2,1)S(1)}, bf16[64,640]{1,0:T(8,128)(2,1)S(1)}, u32[]{:S(2)}, u32[]{:S(2)}) collective-permute-start(bf16[64,640]{1,0:T(8,128)(2,1)S(1)} %pad_maximum_fusion.3.refs_0_), channel_id=1, source_target_pairs={{0,12},{4,8},{8,4},{12,0},{1,13},{5,9},{9,5},{13,1},{2,14},{6,10},... | collective-permute-start | bytes 245768 | tf_op jit(solution)/shard_map/ppermute | solution.py:24
  15.9 1.4 %collective-permute-start.3 = (f32[64,384]{1,0:T(8,128)S(1)}, f32[64,384]{1,0:T(8,128)S(1)}, u32[]{:S(2)}, u32[]{:S(2)}) collective-permute-start(f32[64,384]{1,0:T(8,128)S(1)} %get-tuple-element.37), channel_id=1, source_target_pairs={{0,1},{1,0},{2,3},{3,2},{4,5},{5,4},{6,7},{7,6},{8,9},{9,8},{10,11... | collective-permute-start | bytes 294920 | tf_op jit(solution)/shard_map/ppermute | solution.py:24
  17.3 8.6 %collective-permute-start.4 = (f32[64,384]{1,0:T(8,128)S(1)}, f32[64,384]{1,0:T(8,128)S(1)}, u32[]{:S(2)}, u32[]{:S(2)}) collective-permute-start(f32[64,384]{1,0:T(8,128)S(1)} %add.111), channel_id=1, source_target_pairs={{0,2},{1,3},{2,0},{3,1},{4,6},{5,7},{6,4},{7,5},{8,10},{9,11},{10,... | collective-permute-start | bytes 294920 | tf_op jit(solution)/shard_map/ppermute | solution.py:24
  25.8 7.8 %collective-permute-start.7 = (bf16[2,2,64,512]{3,2,1,0:T(8,128)(2,1)S(1)}, bf16[2,2,64,512]{3,2,1,0:T(8,128)(2,1)S(1)}, u32[]{:S(2)}, u32[]{:S(2)}) collective-permute-start(bf16[2,2,64,512]{3,2,1,0:T(8,128)(2,1)S(1)} %get-tuple-element.40), channel_id=1, source_target_pairs={{0,1},{1,0},{2,3},{3,2},{4,5},{5,4},{6,7},{7,6},{8,9},{9,8},{10,11... | collective-permute-start | bytes 786440 | tf_op jit(solution)/shard_map/ppermute | solution.py:24
  26.3 5.6 %collective-permute-start.5 = (f32[64,128]{1,0:T(8,128)S(1)}, f32[64,128]{1,0:T(8,128)S(1)}, u32[]{:S(2)}, u32[]{:S(2)}) collective-permute-start(f32[64,128]{1,0:T(8,128)S(1)} %get-tuple-element.79), channel_id=1, source_target_pairs={{4,8},{8,4},{5,9},{9,5},{6,10},{10,6},{7,11},{11,7},{20,24},{24,20... | collective-permute-start | bytes 98312 | tf_op jit(solution)/shard_map/ppermute | solution.py:569
  27.0 6.6 %collective-permute-start.6 = (f32[64,128]{1,0:T(8,128)S(1)}, f32[64,128]{1,0:T(8,128)S(1)}, u32[]{:S(2)}, u32[]{:S(2)}) collective-permute-start(f32[64,128]{1,0:T(8,128)S(1)} %get-tuple-element.78), channel_id=1, source_target_pairs={{0,4},{4,12},{8,0},{12,8},{1,5},{5,13},{9,1},{13,9},{2,6},{6,14},{... | collective-permute-start | bytes 98312 | tf_op jit(solution)/shard_map/ppermute | solution.py:568
  33.8 7.6 %collective-permute-start.8 = (bf16[2,64,512]{2,1,0:T(8,128)(2,1)S(1)}, bf16[2,64,512]{2,1,0:T(8,128)(2,1)S(1)}, u32[]{:S(2)}, u32[]{:S(2)}) collective-permute-start(bf16[2,64,512]{2,1,0:T(8,128)(2,1)S(1)} %fusion.21), channel_id=1, source_target_pairs={{0,2},{1,3},{2,0},{3,1},{4,6},{5,7},{6,4},{7,5},{8,10},{9,11},{10,... | collective-permute-start | bytes 393224 | tf_op jit(solution)/shard_map/ppermute | solution.py:24
  42.0 6.1 %collective-permute-start.9 = (bf16[64,640]{1,0:T(8,128)(2,1)S(1)}, bf16[64,640]{1,0:T(8,128)(2,1)S(1)}, u32[]{:S(2)}, u32[]{:S(2)}) collective-permute-start(bf16[64,640]{1,0:T(8,128)(2,1)S(1)} %pad_maximum_fusion.4.refs_0_), channel_id=1, source_target_pairs={{0,1},{1,0},{2,3},{3,2},{4,5},{5,4},{6,7},{7,6},{8,9},{9,8},{10,11... | collective-permute-start | bytes 245768 | tf_op jit(solution)/shard_map/ppermute | solution.py:24
  42.1 6.1 %collective-permute-start.10 = (bf16[64,640]{1,0:T(8,128)(2,1)S(1)}, bf16[64,640]{1,0:T(8,128)(2,1)S(1)}, u32[]{:S(2)}, u32[]{:S(2)}) collective-permute-start(bf16[64,640]{1,0:T(8,128)(2,1)S(1)} %pad_maximum_fusion.4.refs_0_), channel_id=1, source_target_pairs={{0,2},{1,3},{2,0},{3,1},{4,6},{5,7},{6,4},{7,5},{8,10},{9,11},{10,... | collective-permute-start | bytes 245768 | tf_op jit(solution)/shard_map/ppermute | solution.py:24
  43.6 4.7 %collective-permute-start.11 = (bf16[64,640]{1,0:T(8,128)(2,1)S(1)}, bf16[64,640]{1,0:T(8,128)(2,1)S(1)}, u32[]{:S(2)}, u32[]{:S(2)}) collective-permute-start(bf16[64,640]{1,0:T(8,128)(2,1)S(1)} %pad_maximum_fusion.4.refs_0_), channel_id=1, source_target_pairs={{0,3},{1,2},{2,1},{3,0},{4,7},{5,6},{6,5},{7,4},{8,11},{9,10},{10,... | collective-permute-start | bytes 245768 | tf_op jit(solution)/shard_map/ppermute | solution.py:24
  50.5 11.9 %collective-permute-start.12 = (bf16[64,512]{1,0:T(8,128)(2,1)S(1)}, bf16[64,512]{1,0:T(8,128)(2,1)S(1)}, u32[]{:S(2)}, u32[]{:S(2)}) collective-permute-start(bf16[64,512]{1,0:T(8,128)(2,1)S(1)} %get-tuple-element.43), channel_id=1, source_target_pairs={{0,12},{4,8},{8,4},{12,0},{1,13},{5,9},{9,5},{13,1},{2,14},{6,10},... | collective-permute-start | bytes 196616 | tf_op jit(solution)/shard_map/ppermute | solution.py:24
  53.0 9.4 %collective-permute-start.13 = (bf16[64,512]{1,0:T(8,128)(2,1)S(1)}, bf16[64,512]{1,0:T(8,128)(2,1)S(1)}, u32[]{:S(2)}, u32[]{:S(2)}) collective-permute-start(bf16[64,512]{1,0:T(8,128)(2,1)S(1)} %get-tuple-element.44), channel_id=1, source_target_pairs={{0,8},{4,12},{8,0},{12,4},{1,9},{5,13},{9,1},{13,5},{2,10},{6,14},... | collective-permute-start | bytes 196616 | tf_op jit(solution)/shard_map/ppermute | solution.py:24
  53.6 8.8 %collective-permute-start.14 = (bf16[64,512]{1,0:T(8,128)(2,1)S(1)}, bf16[64,512]{1,0:T(8,128)(2,1)S(1)}, u32[]{:S(2)}, u32[]{:S(2)}) collective-permute-start(bf16[64,512]{1,0:T(8,128)(2,1)S(1)} %get-tuple-element.45), channel_id=1, source_target_pairs={{0,4},{4,0},{8,12},{12,8},{1,5},{5,1},{9,13},{13,9},{2,6},{6,2},{1... | collective-permute-start | bytes 196616 | tf_op jit(solution)/shard_map/ppermute | solution.py:24
  62.7 10.5 %collective-permute-start.15 = (bf16[64,640]{1,0:T(8,128)(2,1)S(1)}, bf16[64,640]{1,0:T(8,128)(2,1)S(1)}, u32[]{:S(2)}, u32[]{:S(2)}) collective-permute-start(bf16[64,640]{1,0:T(8,128)(2,1)S(1)} %pad_maximum_fusion.5.refs_0_), channel_id=1, source_target_pairs={{0,4},{4,0},{8,12},{12,8},{1,5},{5,1},{9,13},{13,9},{2,6},{6,2},{1... | collective-permute-start | bytes 245768 | tf_op jit(solution)/shard_map/ppermute | solution.py:24
  63.5 9.7 %collective-permute-start.16 = (bf16[64,640]{1,0:T(8,128)(2,1)S(1)}, bf16[64,640]{1,0:T(8,128)(2,1)S(1)}, u32[]{:S(2)}, u32[]{:S(2)}) collective-permute-start(bf16[64,640]{1,0:T(8,128)(2,1)S(1)} %pad_maximum_fusion.5.refs_0_), channel_id=1, source_target_pairs={{0,8},{4,12},{8,0},{12,4},{1,9},{5,13},{9,1},{13,5},{2,10},{6,14},... | collective-permute-start | bytes 245768 | tf_op jit(solution)/shard_map/ppermute | solution.py:24
  65.8 7.4 %collective-permute-start.17 = (bf16[64,640]{1,0:T(8,128)(2,1)S(1)}, bf16[64,640]{1,0:T(8,128)(2,1)S(1)}, u32[]{:S(2)}, u32[]{:S(2)}) collective-permute-start(bf16[64,640]{1,0:T(8,128)(2,1)S(1)} %pad_maximum_fusion.5.refs_0_), channel_id=1, source_target_pairs={{0,12},{4,8},{8,4},{12,0},{1,13},{5,9},{9,5},{13,1},{2,14},{6,10},... | collective-permute-start | bytes 245768 | tf_op jit(solution)/shard_map/ppermute | solution.py:24
  76.8 1.6 %collective-permute-start.18 = (bf16[64,2176]{1,0:T(8,128)(2,1)S(1)}, bf16[64,2176]{1,0:T(8,128)(2,1)S(1)}, u32[]{:S(2)}, u32[]{:S(2)}) collective-permute-start(bf16[64,2176]{1,0:T(8,128)(2,1)S(1)} %get-tuple-element.52), channel_id=1, source_target_pairs={{0,1},{1,0},{2,3},{3,2},{4,5},{5,4},{6,7},{7,6},{8,9},{9,8},{10,11... | collective-permute-start | bytes 835592 | tf_op jit(solution)/shard_map/ppermute | solution.py:24
  79.0 8.8 %collective-permute-start.19 = (bf16[64,2176]{1,0:T(8,128)(2,1)S(1)}, bf16[64,2176]{1,0:T(8,128)(2,1)S(1)}, u32[]{:S(2)}, u32[]{:S(2)}) collective-permute-start(bf16[64,2176]{1,0:T(8,128)(2,1)S(1)} %pad_maximum_fusion.2), channel_id=1, source_target_pairs={{0,2},{1,3},{2,0},{3,1},{4,6},{5,7},{6,4},{7,5},{8,10},{9,11},{10,... | collective-permute-start | bytes 835592 | tf_op jit(solution)/shard_map/ppermute | solution.py:24
  88.3 1.6 %collective-permute-start.20 = (bf16[64,2048]{1,0:T(8,128)(2,1)S(1)}, bf16[64,2048]{1,0:T(8,128)(2,1)S(1)}, u32[]{:S(2)}, u32[]{:S(2)}) collective-permute-start(bf16[64,2048]{1,0:T(8,128)(2,1)S(1)} %multiply_convert_fusion.first), channel_id=1, source_target_pairs={{0,1},{1,0},{2,3},{3,2},{4,5},{5,4},{6,7},{7,6},{8,9},{9,8},{10,11... | collective-permute-start | bytes 786440 | tf_op jit(solution)/shard_map/ppermute | solution.py:24
  93.5 12.7 %collective-permute-start.21 = (bf16[64,512]{1,0:T(8,128)(2,1)S(1)}, bf16[64,512]{1,0:T(8,128)(2,1)S(1)}, u32[]{:S(2)}, u32[]{:S(2)}) collective-permute-start(bf16[64,512]{1,0:T(8,128)(2,1)S(1)} %get-tuple-element.57), channel_id=1, source_target_pairs={{0,12},{4,8},{8,4},{12,0},{1,13},{5,9},{9,5},{13,1},{2,14},{6,10},... | collective-permute-start | bytes 196616 | tf_op jit(solution)/shard_map/ppermute | solution.py:24
  96.0 10.2 %collective-permute-start.22 = (bf16[64,512]{1,0:T(8,128)(2,1)S(1)}, bf16[64,512]{1,0:T(8,128)(2,1)S(1)}, u32[]{:S(2)}, u32[]{:S(2)}) collective-permute-start(bf16[64,512]{1,0:T(8,128)(2,1)S(1)} %get-tuple-element.58), channel_id=1, source_target_pairs={{0,8},{4,12},{8,0},{12,4},{1,9},{5,13},{9,1},{13,5},{2,10},{6,14},... | collective-permute-start | bytes 196616 | tf_op jit(solution)/shard_map/ppermute | solution.py:24
  96.0 10.2 %collective-permute-start.23 = (bf16[64,512]{1,0:T(8,128)(2,1)S(1)}, bf16[64,512]{1,0:T(8,128)(2,1)S(1)}, u32[]{:S(2)}, u32[]{:S(2)}) collective-permute-start(bf16[64,512]{1,0:T(8,128)(2,1)S(1)} %get-tuple-element.59), channel_id=1, source_target_pairs={{0,4},{4,0},{8,12},{12,8},{1,5},{5,1},{9,13},{13,9},{2,6},{6,2},{1... | collective-permute-start | bytes 196616 | tf_op jit(solution)/shard_map/ppermute | solution.py:24
  (10 other events, 163.0 us)

commit v4 on v3

--- a/solution.py
+++ b/solution.py
@@ -439,7 +439,7 @@
 def update_body(first, rows, decay, state, inputs, state_in, *refs):
     target, held, across, arrived, sent = refs[-5:]
     _, heads, size, _ = state.shape
-    step, together = 4, 4
+    step, together = 2, 8
     pieces = rows // step
     come = started(
         (state.at[pl.ds(first + i * step, step)], held.at[pl.ds(i * step, step)], arrived.at[i]) for i in range(pieces)
@@ -472,7 +472,7 @@
     if before is not None:
         given.append(before)
         specs.append(IN_PLACE)
-    pieces = rows // 4
+    pieces = rows // 2
     return pl.pallas_call(
         functools.partial(update_body, first, rows),
         in_specs=specs,

time: 107 us -> 107 us (level)
  transfers between devices with their start and end apart: 24 -> 24, of which waited for: 7 -> 6; matrix products, arithmetic and copies ran while one was open for 5% -> 5% of each run, Pallas kernels for 39% -> 39%
where the time goes in v4:
time: 107 us
  Pallas kernels  52.1 us (49%)
  starting transfers between devices  29.9 us (28%)
  waiting for transfers between devices  8.56 us (8%)
  other arithmetic  8.04 us (8%)
  local copies, waits for them, and re-layouts  6.94 us (6%)
  between operations  1.23 us (1%)
    ppermute x22, starting transfers between devices, swap(): return lax.ppermute(value, axis, [(i, i ^ bits) for i in range(size)])  24.9 us
    pallas_call x5, Pallas kernels, call(): pl.pallas_call(body, in_specs=[IN_SMEM] + [IN_VMEM] * len(arrays) + [IN_P...  17.4 us
    pallas_call x2, Pallas kernels, updated(): pl.pallas_call(functools.partial(update_body, first, rows), in_specs=spec...  14.8 us
    pallas_call x5, Pallas kernels, fetched(): pl.pallas_call(functools.partial(fetch_body, pieces), in_specs=[pl.BlockS...  12.9 us
    pallas_call x1, Pallas kernels, state_products(): pl.pallas_call(functools.partial(product_body, step), in_specs=[IN_PLACE,...  7 us
    ppermute x22, waiting for transfers between devices, swap(): return lax.ppermute(value, axis, [(i, i ^ bits) for i in range(size)])  6.92 us
    unnamed x20, local copies, waits for them, and re-layouts  5.53 us
    ppermute x1, starting transfers between devices, fast(): lax.ppermute(jnp.where(at_long < 2, high, low), 'long', [(0, 1), (1, 3),...  4.32 us
  transfers between devices with their start and end apart: 24, of which 6 were waited for; matrix products, arithmetic and copies ran while one was open for 5% of the time, Pallas kernels for 39%

profile of v4, /device:TPU:0, one launch (start us, length us, event | category | flops | bytes accessed | tf_op | source)
XLA Modules:
  0.0 106.8 jit_solution(1699530297105622640)
XLA Ops:
  2.5 3.1 %collective-permute-start = (bf16[64,640]{1,0:T(8,128)(2,1)S(1)}, bf16[64,640]{1,0:T(8,128)(2,1)S(1)}, u32[]{:S(2)}, u32[]{:S(2)}) collective-permute-start(bf16[64,640]{1,0:T(8,128)(2,1)S(1)} %pad_maximum_fusion.3.refs_0_), channel_id=1, source_target_pairs={{0,4},{4,0},{8,12},{12,8},{1,5},{5,1},{9,13},{13,9},{2,6},{6,2},{1... | collective-permute-start | bytes 245768 | tf_op jit(solution)/shard_map/ppermute | solution.py:24
  5.6 2.6 %collective-permute-start.1 = (bf16[64,640]{1,0:T(8,128)(2,1)S(1)}, bf16[64,640]{1,0:T(8,128)(2,1)S(1)}, u32[]{:S(2)}, u32[]{:S(2)}) collective-permute-start(bf16[64,640]{1,0:T(8,128)(2,1)S(1)} %pad_maximum_fusion.3.refs_0_), channel_id=1, source_target_pairs={{0,8},{4,12},{8,0},{12,4},{1,9},{5,13},{9,1},{13,5},{2,10},{6,14},... | collective-permute-start | bytes 245768 | tf_op jit(solution)/shard_map/ppermute | solution.py:24
  12.7 2.1 %collective-permute-done.1.refs_2_ = bf16[64,640]{1,0:T(8,128)(2,1)S(1)} collective-permute-done((bf16[64,640]{1,0:T(8,128)(2,1)S(1)}, bf16[64,640]{1,0:T(8,128)(2,1)S(1)}, u32[]{:S(2)}, u32[]{:S(2)}) %collective-permute-start.1) | collective-permute-done | bytes 81952 | tf_op jit(solution)/shard_map/ppermute | solution.py:24
  17.3 1.6 %collective-permute-start.4 = (f32[64,384]{1,0:T(8,128)S(1)}, f32[64,384]{1,0:T(8,128)S(1)}, u32[]{:S(2)}, u32[]{:S(2)}) collective-permute-start(f32[64,384]{1,0:T(8,128)S(1)} %add.111), channel_id=1, source_target_pairs={{0,2},{1,3},{2,0},{3,1},{4,6},{5,7},{6,4},{7,5},{8,10},{9,11},{10,... | collective-permute-start | bytes 294920 | tf_op jit(solution)/shard_map/ppermute | solution.py:24
  18.9 7.0 %gates.1 = (f32[2,2,64,512]{3,2,1,0:T(8,128)S(1)}, bf16[2,2,64,512]{3,2,1,0:T(8,128)(2,1)S(1)}) custom-call(s32[3]{0:T(128)S(1)} %pad_add_fusion.1.place, bf16[4,128,1024]{2,1,0:T(8,128)(2,1)S(1)} %get-tuple-element.38.spread, bf16[2048,2,2048]{2,1,0:T(2,128)(2,1)} %weight.1), custom_call_target="tpu_custom_call" | custom-call | flops 2147483648 | bytes 17825792 | tf_op jit(solution)/shard_map/gates/pallas_call | solution.py:221
  27.0 4.3 %collective-permute-start.6 = (f32[64,128]{1,0:T(8,128)S(1)}, f32[64,128]{1,0:T(8,128)S(1)}, u32[]{:S(2)}, u32[]{:S(2)}) collective-permute-start(f32[64,128]{1,0:T(8,128)S(1)} %get-tuple-element.78), channel_id=1, source_target_pairs={{0,4},{4,12},{8,0},{12,8},{1,5},{5,13},{9,1},{13,9},{2,6},{6,14},{... | collective-permute-start | bytes 98312 | tf_op jit(solution)/shard_map/ppermute | solution.py:568
  31.9 1.6 %collective-permute-done.6 = f32[64,128]{1,0:T(8,128)S(1)} collective-permute-done((f32[64,128]{1,0:T(8,128)S(1)}, f32[64,128]{1,0:T(8,128)S(1)}, u32[]{:S(2)}, u32[]{:S(2)}) %collective-permute-start.6) | collective-permute-done | bytes 32800 | tf_op jit(solution)/shard_map/ppermute | solution.py:568
  34.4 7.0 %state_products.1 = f32[64,512]{1,0:T(8,128)S(1)} custom-call(f32[64,8,64,128]{3,2,1,0:T(8,128)} %state.3, f32[64,128]{1,0:T(8,128)S(1)} %get-tuple-element.85.out_hi, f32[64,128]{1,0:T(8,128)S(1)} %get-tuple-element.84.out_lo), custom_call_target="tpu_custom_call" | custom-call | flops 268435456 | bytes 16777216 | tf_op jit(solution)/shard_map/state_products/pallas_call | solution.py:427
  42.1 1.6 %collective-permute-start.10 = (bf16[64,640]{1,0:T(8,128)(2,1)S(1)}, bf16[64,640]{1,0:T(8,128)(2,1)S(1)}, u32[]{:S(2)}, u32[]{:S(2)}) collective-permute-start(bf16[64,640]{1,0:T(8,128)(2,1)S(1)} %pad_maximum_fusion.4.refs_0_), channel_id=1, source_target_pairs={{0,2},{1,3},{2,0},{3,1},{4,6},{5,7},{6,4},{7,5},{8,10},{9,11},{10,... | collective-permute-start | bytes 245768 | tf_op jit(solution)/shard_map/ppermute | solution.py:24
  44.1 3.4 %copy-done = bf16[2048,2048]{1,0:T(8,128)(2,1)S(1)} copy-done((bf16[2048,2048]{1,0:T(8,128)(2,1)S(1)}, bf16[2048,2048]{1,0:T(8,128)(2,1)}, u32[]{:S(2)}) %copy-start) | copy-done | bytes 8388632
  48.4 2.1 %mixed.1 = (f32[64,512]{1,0:T(8,128)S(1)}, bf16[64,512]{1,0:T(8,128)(2,1)S(1)}, bf16[64,512]{1,0:T(8,128)(2,1)S(1)}, bf16[64,512]{1,0:T(8,128)(2,1)S(1)}) custom-call(s32[2]{0:T(128)S(1)} %pad_add_fusion.place, bf16[64,640]{1,0:T(8,128)(2,1)S(1)} %pad_maximum_fusion.4.refs_0_, bf16[64,640]{1,0:T(8,128)(2,1)S(1)} %collective-permute-done.9.refs_1_, ...), custom_call_target="tpu_custom_call" | custom-call | flops 536870912 | bytes 8716288 | tf_op jit(solution)/shard_map/mixed/pallas_call | solution.py:221
  50.5 2.5 %collective-permute-start.12 = (bf16[64,512]{1,0:T(8,128)(2,1)S(1)}, bf16[64,512]{1,0:T(8,128)(2,1)S(1)}, u32[]{:S(2)}, u32[]{:S(2)}) collective-permute-start(bf16[64,512]{1,0:T(8,128)(2,1)S(1)} %get-tuple-element.43), channel_id=1, source_target_pairs={{0,12},{4,8},{8,4},{12,0},{1,13},{5,9},{9,5},{13,1},{2,14},{6,10},... | collective-permute-start | bytes 196616 | tf_op jit(solution)/shard_map/ppermute | solution.py:24
  54.9 7.4 %update_first.1.refs_0_ = f32[64,8,64,128]{3,2,1,0:T(8,128)} custom-call(f32[512]{0:T(512)S(1)} %reshape.56.decay, f32[64,8,64,128]{3,2,1,0:T(8,128)} %state.3, f32[64,512]{1,0:T(8,128)S(1)} %get-tuple-element.77.inputs, f32[32,128]{1,0:T(8,128)S(1)} %get-tuple-element.83.state_in), custom_call_target="tpu_custom_call" | custom-call | flops 6291456 | bytes 16777216 | tf_op jit(solution)/shard_map/update_first/pallas_call | solution.py:476
  63.5 2.3 %collective-permute-start.16 = (bf16[64,640]{1,0:T(8,128)(2,1)S(1)}, bf16[64,640]{1,0:T(8,128)(2,1)S(1)}, u32[]{:S(2)}, u32[]{:S(2)}) collective-permute-start(bf16[64,640]{1,0:T(8,128)(2,1)S(1)} %pad_maximum_fusion.5.refs_0_), channel_id=1, source_target_pairs={{0,8},{4,12},{8,0},{12,4},{1,9},{5,13},{9,1},{13,5},{2,10},{6,14},... | collective-permute-start | bytes 245768 | tf_op jit(solution)/shard_map/ppermute | solution.py:24
  65.8 1.4 %collective-permute-start.17 = (bf16[64,640]{1,0:T(8,128)(2,1)S(1)}, bf16[64,640]{1,0:T(8,128)(2,1)S(1)}, u32[]{:S(2)}, u32[]{:S(2)}) collective-permute-start(bf16[64,640]{1,0:T(8,128)(2,1)S(1)} %pad_maximum_fusion.5.refs_0_), channel_id=1, source_target_pairs={{0,12},{4,8},{8,4},{12,0},{1,13},{5,9},{9,5},{13,1},{2,14},{6,10},... | collective-permute-start | bytes 245768 | tf_op jit(solution)/shard_map/ppermute | solution.py:24
  67.2 5.9 %fetch_upward.1.refs_4_ = bf16[2048,4096]{1,0:T(8,128)(2,1)S(1)} custom-call(bf16[2048,4096]{1,0:T(8,128)(2,1)} %source.2), custom_call_target="tpu_custom_call" | custom-call | bytes 33554432 | tf_op jit(solution)/shard_map/fetch_upward/pallas_call | solution.py:254
  73.2 3.6 %upward.1 = (f32[64,2176]{1,0:T(8,128)S(1)}, bf16[64,2176]{1,0:T(8,128)(2,1)S(1)}) custom-call(s32[2]{0:T(128)S(1)} %pad_add_fusion.3.place, bf16[64,640]{1,0:T(8,128)(2,1)S(1)} %pad_maximum_fusion.5.refs_0_, bf16[64,640]{1,0:T(8,128)(2,1)S(1)} %collective-permute-done.15.refs_1_, bf16[64,640]{1,0:T(8,128)(2,1)S(1)} %collective-permute-done.16.refs_2_, ...), custom_call_target="tpu_custom_call" | custom-call | flops 1073741824 | bytes 17104896 | tf_op jit(solution)/shard_map/upward/pallas_call | solution.py:221
  76.8 1.5 %collective-permute-done.18 = bf16[64,2176]{1,0:T(8,128)(2,1)S(1)} collective-permute-done((bf16[64,2176]{1,0:T(8,128)(2,1)S(1)}, bf16[64,2176]{1,0:T(8,128)(2,1)S(1)}, u32[]{:S(2)}, u32[]{:S(2)}) %collective-permute-start.18) | collective-permute-done | bytes 278560 | tf_op jit(solution)/shard_map/ppermute | solution.py:24
  78.9 1.5 %collective-permute-start.19 = (bf16[64,2176]{1,0:T(8,128)(2,1)S(1)}, bf16[64,2176]{1,0:T(8,128)(2,1)S(1)}, u32[]{:S(2)}, u32[]{:S(2)}) collective-permute-start(bf16[64,2176]{1,0:T(8,128)(2,1)S(1)} %pad_maximum_fusion.2), channel_id=1, source_target_pairs={{0,2},{1,3},{2,0},{3,1},{4,6},{5,7},{6,4},{7,5},{8,10},{9,11},{10,... | collective-permute-start | bytes 835592 | tf_op jit(solution)/shard_map/ppermute | solution.py:24
  80.5 5.9 %fetch_downward.1.weight = bf16[4096,2048]{1,0:T(8,128)(2,1)S(1)} custom-call(bf16[4096,2048]{1,0:T(8,128)(2,1)} %source.3), custom_call_target="tpu_custom_call" | custom-call | bytes 33554432 | tf_op jit(solution)/shard_map/fetch_downward/pallas_call | solution.py:254
  89.8 3.6 %downward.1 = (f32[64,512]{1,0:T(8,128)S(1)}, bf16[64,512]{1,0:T(8,128)(2,1)S(1)}, bf16[64,512]{1,0:T(8,128)(2,1)S(1)}, bf16[64,512]{1,0:T(8,128)(2,1)S(1)}) custom-call(s32[2]{0:T(128)S(1)} %pad_add_fusion.2.place, bf16[64,2048]{1,0:T(8,128)(2,1)S(1)} %multiply_convert_fusion.first, bf16[64,2048]{1,0:T(8,128)(2,1)S(1)} %collective-permute-done.20.second, ...), custom_call_target="tpu_custom_call" | custom-call | flops 1073741824 | bytes 17301504 | tf_op jit(solution)/shard_map/downward/pallas_call | solution.py:221
  93.4 2.5 %collective-permute-start.21 = (bf16[64,512]{1,0:T(8,128)(2,1)S(1)}, bf16[64,512]{1,0:T(8,128)(2,1)S(1)}, u32[]{:S(2)}, u32[]{:S(2)}) collective-permute-start(bf16[64,512]{1,0:T(8,128)(2,1)S(1)} %get-tuple-element.57), channel_id=1, source_target_pairs={{0,12},{4,8},{8,4},{12,0},{1,13},{5,9},{9,5},{13,1},{2,14},{6,10},... | collective-permute-start | bytes 196616 | tf_op jit(solution)/shard_map/ppermute | solution.py:24
  96.0 1.9 %collective-permute-start.23 = (bf16[64,512]{1,0:T(8,128)(2,1)S(1)}, bf16[64,512]{1,0:T(8,128)(2,1)S(1)}, u32[]{:S(2)}, u32[]{:S(2)}) collective-permute-start(bf16[64,512]{1,0:T(8,128)(2,1)S(1)} %get-tuple-element.59), channel_id=1, source_target_pairs={{0,4},{4,0},{8,12},{12,8},{1,5},{5,1},{9,13},{13,9},{2,6},{6,2},{1... | collective-permute-start | bytes 196616 | tf_op jit(solution)/shard_map/ppermute | solution.py:24
  98.7 7.4 %update_last.1 = f32[64,8,64,128]{3,2,1,0:T(8,128)} custom-call(f32[512]{0:T(512)S(1)} %reshape.56.decay, f32[64,8,64,128]{3,2,1,0:T(8,128)} %state.3, f32[64,512]{1,0:T(8,128)S(1)} %get-tuple-element.77.inputs, f32[32,128]{1,0:T(8,128)S(1)} %get-tuple-element.82.state_in, f32[64,8,64,128]{3,2,1,0:T(8,128)} %update_first.1.refs_0_), custom_call_target="tpu_custom_call", output_to_operand_aliasing={{}: (4, {})} | custom-call | flops 6291456 | bytes 16777216 | tf_op jit(solution)/shard_map/update_last/pallas_call | solution.py:476
  (114 shorter events, 21.7 us)
Async XLA Ops:
  2.5 10.2 %collective-permute-start = (bf16[64,640]{1,0:T(8,128)(2,1)S(1)}, bf16[64,640]{1,0:T(8,128)(2,1)S(1)}, u32[]{:S(2)}, u32[]{:S(2)}) collective-permute-start(bf16[64,640]{1,0:T(8,128)(2,1)S(1)} %pad_maximum_fusion.3.refs_0_), channel_id=1, source_target_pairs={{0,4},{4,0},{8,12},{12,8},{1,5},{5,1},{9,13},{13,9},{2,6},{6,2},{1... | collective-permute-start | bytes 245768 | tf_op jit(solution)/shard_map/ppermute | solution.py:24
  5.6 9.2 %collective-permute-start.1 = (bf16[64,640]{1,0:T(8,128)(2,1)S(1)}, bf16[64,640]{1,0:T(8,128)(2,1)S(1)}, u32[]{:S(2)}, u32[]{:S(2)}) collective-permute-start(bf16[64,640]{1,0:T(8,128)(2,1)S(1)} %pad_maximum_fusion.3.refs_0_), channel_id=1, source_target_pairs={{0,8},{4,12},{8,0},{12,4},{1,9},{5,13},{9,1},{13,5},{2,10},{6,14},... | collective-permute-start | bytes 245768 | tf_op jit(solution)/shard_map/ppermute | solution.py:24
  8.2 6.6 %collective-permute-start.2 = (bf16[64,640]{1,0:T(8,128)(2,1)S(1)}, bf16[64,640]{1,0:T(8,128)(2,1)S(1)}, u32[]{:S(2)}, u32[]{:S(2)}) collective-permute-start(bf16[64,640]{1,0:T(8,128)(2,1)S(1)} %pad_maximum_fusion.3.refs_0_), channel_id=1, source_target_pairs={{0,12},{4,8},{8,4},{12,0},{1,13},{5,9},{9,5},{13,1},{2,14},{6,10},... | collective-permute-start | bytes 245768 | tf_op jit(solution)/shard_map/ppermute | solution.py:24
  15.9 1.4 %collective-permute-start.3 = (f32[64,384]{1,0:T(8,128)S(1)}, f32[64,384]{1,0:T(8,128)S(1)}, u32[]{:S(2)}, u32[]{:S(2)}) collective-permute-start(f32[64,384]{1,0:T(8,128)S(1)} %get-tuple-element.37), channel_id=1, source_target_pairs={{0,1},{1,0},{2,3},{3,2},{4,5},{5,4},{6,7},{7,6},{8,9},{9,8},{10,11... | collective-permute-start | bytes 294920 | tf_op jit(solution)/shard_map/ppermute | solution.py:24
  17.3 8.6 %collective-permute-start.4 = (f32[64,384]{1,0:T(8,128)S(1)}, f32[64,384]{1,0:T(8,128)S(1)}, u32[]{:S(2)}, u32[]{:S(2)}) collective-permute-start(f32[64,384]{1,0:T(8,128)S(1)} %add.111), channel_id=1, source_target_pairs={{0,2},{1,3},{2,0},{3,1},{4,6},{5,7},{6,4},{7,5},{8,10},{9,11},{10,... | collective-permute-start | bytes 294920 | tf_op jit(solution)/shard_map/ppermute | solution.py:24
  25.8 7.8 %collective-permute-start.7 = (bf16[2,2,64,512]{3,2,1,0:T(8,128)(2,1)S(1)}, bf16[2,2,64,512]{3,2,1,0:T(8,128)(2,1)S(1)}, u32[]{:S(2)}, u32[]{:S(2)}) collective-permute-start(bf16[2,2,64,512]{3,2,1,0:T(8,128)(2,1)S(1)} %get-tuple-element.40), channel_id=1, source_target_pairs={{0,1},{1,0},{2,3},{3,2},{4,5},{5,4},{6,7},{7,6},{8,9},{9,8},{10,11... | collective-permute-start | bytes 786440 | tf_op jit(solution)/shard_map/ppermute | solution.py:24
  26.3 5.6 %collective-permute-start.5 = (f32[64,128]{1,0:T(8,128)S(1)}, f32[64,128]{1,0:T(8,128)S(1)}, u32[]{:S(2)}, u32[]{:S(2)}) collective-permute-start(f32[64,128]{1,0:T(8,128)S(1)} %get-tuple-element.79), channel_id=1, source_target_pairs={{4,8},{8,4},{5,9},{9,5},{6,10},{10,6},{7,11},{11,7},{20,24},{24,20... | collective-permute-start | bytes 98312 | tf_op jit(solution)/shard_map/ppermute | solution.py:569
  27.0 6.6 %collective-permute-start.6 = (f32[64,128]{1,0:T(8,128)S(1)}, f32[64,128]{1,0:T(8,128)S(1)}, u32[]{:S(2)}, u32[]{:S(2)}) collective-permute-start(f32[64,128]{1,0:T(8,128)S(1)} %get-tuple-element.78), channel_id=1, source_target_pairs={{0,4},{4,12},{8,0},{12,8},{1,5},{5,13},{9,1},{13,9},{2,6},{6,14},{... | collective-permute-start | bytes 98312 | tf_op jit(solution)/shard_map/ppermute | solution.py:568
  33.8 7.6 %collective-permute-start.8 = (bf16[2,64,512]{2,1,0:T(8,128)(2,1)S(1)}, bf16[2,64,512]{2,1,0:T(8,128)(2,1)S(1)}, u32[]{:S(2)}, u32[]{:S(2)}) collective-permute-start(bf16[2,64,512]{2,1,0:T(8,128)(2,1)S(1)} %fusion.21), channel_id=1, source_target_pairs={{0,2},{1,3},{2,0},{3,1},{4,6},{5,7},{6,4},{7,5},{8,10},{9,11},{10,... | collective-permute-start | bytes 393224 | tf_op jit(solution)/shard_map/ppermute | solution.py:24
  42.0 6.3 %collective-permute-start.9 = (bf16[64,640]{1,0:T(8,128)(2,1)S(1)}, bf16[64,640]{1,0:T(8,128)(2,1)S(1)}, u32[]{:S(2)}, u32[]{:S(2)}) collective-permute-start(bf16[64,640]{1,0:T(8,128)(2,1)S(1)} %pad_maximum_fusion.4.refs_0_), channel_id=1, source_target_pairs={{0,1},{1,0},{2,3},{3,2},{4,5},{5,4},{6,7},{7,6},{8,9},{9,8},{10,11... | collective-permute-start | bytes 245768 | tf_op jit(solution)/shard_map/ppermute | solution.py:24
  42.1 6.3 %collective-permute-start.10 = (bf16[64,640]{1,0:T(8,128)(2,1)S(1)}, bf16[64,640]{1,0:T(8,128)(2,1)S(1)}, u32[]{:S(2)}, u32[]{:S(2)}) collective-permute-start(bf16[64,640]{1,0:T(8,128)(2,1)S(1)} %pad_maximum_fusion.4.refs_0_), channel_id=1, source_target_pairs={{0,2},{1,3},{2,0},{3,1},{4,6},{5,7},{6,4},{7,5},{8,10},{9,11},{10,... | collective-permute-start | bytes 245768 | tf_op jit(solution)/shard_map/ppermute | solution.py:24
  43.6 4.7 %collective-permute-start.11 = (bf16[64,640]{1,0:T(8,128)(2,1)S(1)}, bf16[64,640]{1,0:T(8,128)(2,1)S(1)}, u32[]{:S(2)}, u32[]{:S(2)}) collective-permute-start(bf16[64,640]{1,0:T(8,128)(2,1)S(1)} %pad_maximum_fusion.4.refs_0_), channel_id=1, source_target_pairs={{0,3},{1,2},{2,1},{3,0},{4,7},{5,6},{6,5},{7,4},{8,11},{9,10},{10,... | collective-permute-start | bytes 245768 | tf_op jit(solution)/shard_map/ppermute | solution.py:24
  50.5 11.9 %collective-permute-start.12 = (bf16[64,512]{1,0:T(8,128)(2,1)S(1)}, bf16[64,512]{1,0:T(8,128)(2,1)S(1)}, u32[]{:S(2)}, u32[]{:S(2)}) collective-permute-start(bf16[64,512]{1,0:T(8,128)(2,1)S(1)} %get-tuple-element.43), channel_id=1, source_target_pairs={{0,12},{4,8},{8,4},{12,0},{1,13},{5,9},{9,5},{13,1},{2,14},{6,10},... | collective-permute-start | bytes 196616 | tf_op jit(solution)/shard_map/ppermute | solution.py:24
  53.0 9.4 %collective-permute-start.13 = (bf16[64,512]{1,0:T(8,128)(2,1)S(1)}, bf16[64,512]{1,0:T(8,128)(2,1)S(1)}, u32[]{:S(2)}, u32[]{:S(2)}) collective-permute-start(bf16[64,512]{1,0:T(8,128)(2,1)S(1)} %get-tuple-element.44), channel_id=1, source_target_pairs={{0,8},{4,12},{8,0},{12,4},{1,9},{5,13},{9,1},{13,5},{2,10},{6,14},... | collective-permute-start | bytes 196616 | tf_op jit(solution)/shard_map/ppermute | solution.py:24
  53.6 8.7 %collective-permute-start.14 = (bf16[64,512]{1,0:T(8,128)(2,1)S(1)}, bf16[64,512]{1,0:T(8,128)(2,1)S(1)}, u32[]{:S(2)}, u32[]{:S(2)}) collective-permute-start(bf16[64,512]{1,0:T(8,128)(2,1)S(1)} %get-tuple-element.45), channel_id=1, source_target_pairs={{0,4},{4,0},{8,12},{12,8},{1,5},{5,1},{9,13},{13,9},{2,6},{6,2},{1... | collective-permute-start | bytes 196616 | tf_op jit(solution)/shard_map/ppermute | solution.py:24
  62.7 10.5 %collective-permute-start.15 = (bf16[64,640]{1,0:T(8,128)(2,1)S(1)}, bf16[64,640]{1,0:T(8,128)(2,1)S(1)}, u32[]{:S(2)}, u32[]{:S(2)}) collective-permute-start(bf16[64,640]{1,0:T(8,128)(2,1)S(1)} %pad_maximum_fusion.5.refs_0_), channel_id=1, source_target_pairs={{0,4},{4,0},{8,12},{12,8},{1,5},{5,1},{9,13},{13,9},{2,6},{6,2},{1... | collective-permute-start | bytes 245768 | tf_op jit(solution)/shard_map/ppermute | solution.py:24
  63.5 9.7 %collective-permute-start.16 = (bf16[64,640]{1,0:T(8,128)(2,1)S(1)}, bf16[64,640]{1,0:T(8,128)(2,1)S(1)}, u32[]{:S(2)}, u32[]{:S(2)}) collective-permute-start(bf16[64,640]{1,0:T(8,128)(2,1)S(1)} %pad_maximum_fusion.5.refs_0_), channel_id=1, source_target_pairs={{0,8},{4,12},{8,0},{12,4},{1,9},{5,13},{9,1},{13,5},{2,10},{6,14},... | collective-permute-start | bytes 245768 | tf_op jit(solution)/shard_map/ppermute | solution.py:24
  65.8 7.4 %collective-permute-start.17 = (bf16[64,640]{1,0:T(8,128)(2,1)S(1)}, bf16[64,640]{1,0:T(8,128)(2,1)S(1)}, u32[]{:S(2)}, u32[]{:S(2)}) collective-permute-start(bf16[64,640]{1,0:T(8,128)(2,1)S(1)} %pad_maximum_fusion.5.refs_0_), channel_id=1, source_target_pairs={{0,12},{4,8},{8,4},{12,0},{1,13},{5,9},{9,5},{13,1},{2,14},{6,10},... | collective-permute-start | bytes 245768 | tf_op jit(solution)/shard_map/ppermute | solution.py:24
  76.8 1.6 %collective-permute-start.18 = (bf16[64,2176]{1,0:T(8,128)(2,1)S(1)}, bf16[64,2176]{1,0:T(8,128)(2,1)S(1)}, u32[]{:S(2)}, u32[]{:S(2)}) collective-permute-start(bf16[64,2176]{1,0:T(8,128)(2,1)S(1)} %get-tuple-element.52), channel_id=1, source_target_pairs={{0,1},{1,0},{2,3},{3,2},{4,5},{5,4},{6,7},{7,6},{8,9},{9,8},{10,11... | collective-permute-start | bytes 835592 | tf_op jit(solution)/shard_map/ppermute | solution.py:24
  78.9 8.8 %collective-permute-start.19 = (bf16[64,2176]{1,0:T(8,128)(2,1)S(1)}, bf16[64,2176]{1,0:T(8,128)(2,1)S(1)}, u32[]{:S(2)}, u32[]{:S(2)}) collective-permute-start(bf16[64,2176]{1,0:T(8,128)(2,1)S(1)} %pad_maximum_fusion.2), channel_id=1, source_target_pairs={{0,2},{1,3},{2,0},{3,1},{4,6},{5,7},{6,4},{7,5},{8,10},{9,11},{10,... | collective-permute-start | bytes 835592 | tf_op jit(solution)/shard_map/ppermute | solution.py:24
  88.2 1.6 %collective-permute-start.20 = (bf16[64,2048]{1,0:T(8,128)(2,1)S(1)}, bf16[64,2048]{1,0:T(8,128)(2,1)S(1)}, u32[]{:S(2)}, u32[]{:S(2)}) collective-permute-start(bf16[64,2048]{1,0:T(8,128)(2,1)S(1)} %multiply_convert_fusion.first), channel_id=1, source_target_pairs={{0,1},{1,0},{2,3},{3,2},{4,5},{5,4},{6,7},{7,6},{8,9},{9,8},{10,11... | collective-permute-start | bytes 786440 | tf_op jit(solution)/shard_map/ppermute | solution.py:24
  93.4 12.6 %collective-permute-start.21 = (bf16[64,512]{1,0:T(8,128)(2,1)S(1)}, bf16[64,512]{1,0:T(8,128)(2,1)S(1)}, u32[]{:S(2)}, u32[]{:S(2)}) collective-permute-start(bf16[64,512]{1,0:T(8,128)(2,1)S(1)} %get-tuple-element.57), channel_id=1, source_target_pairs={{0,12},{4,8},{8,4},{12,0},{1,13},{5,9},{9,5},{13,1},{2,14},{6,10},... | collective-permute-start | bytes 196616 | tf_op jit(solution)/shard_map/ppermute | solution.py:24
  96.0 10.1 %collective-permute-start.22 = (bf16[64,512]{1,0:T(8,128)(2,1)S(1)}, bf16[64,512]{1,0:T(8,128)(2,1)S(1)}, u32[]{:S(2)}, u32[]{:S(2)}) collective-permute-start(bf16[64,512]{1,0:T(8,128)(2,1)S(1)} %get-tuple-element.58), channel_id=1, source_target_pairs={{0,8},{4,12},{8,0},{12,4},{1,9},{5,13},{9,1},{13,5},{2,10},{6,14},... | collective-permute-start | bytes 196616 | tf_op jit(solution)/shard_map/ppermute | solution.py:24
  96.0 10.1 %collective-permute-start.23 = (bf16[64,512]{1,0:T(8,128)(2,1)S(1)}, bf16[64,512]{1,0:T(8,128)(2,1)S(1)}, u32[]{:S(2)}, u32[]{:S(2)}) collective-permute-start(bf16[64,512]{1,0:T(8,128)(2,1)S(1)} %get-tuple-element.59), channel_id=1, source_target_pairs={{0,4},{4,0},{8,12},{12,8},{1,5},{5,1},{9,13},{13,9},{2,6},{6,2},{1... | collective-permute-start | bytes 196616 | tf_op jit(solution)/shard_map/ppermute | solution.py:24
  (10 other events, 163.0 us)
